TPU v7x, 512 devices: a whole 4x4x16 slice. The times are simulated.
512 devices in a mesh: graph: 16 (over z), row: 32 (over x, y, core).
Axes of the slice: x: 4, y: 4, z: 16, core: 2. Of those that a mesh axis runs over, the one named last changes fastest.
Arguments:
- pair: bfloat16 [6144, 384, 128], P(('graph', 'row')), parts along dimension 0, may hold values from -6 to 6
- edge_type: int32 [6144, 384], P(('graph', 'row')), parts along dimension 0, may hold values from 0 to 7
- node_mask: int32 [6144], P('graph'), parts along dimension 0, may hold values 0 or 1
- type_table: bfloat16 [8, 128], replicated, may hold values from -6 to 6
- in_gain: float32 [2, 128], replicated, may hold values from 0.1 to 1.9
- proj_weight: bfloat16 [2, 128, 512], replicated, may hold values from -0.5 to 0.5
- gate_weight: bfloat16 [2, 128, 128], replicated, may hold values from -0.5 to 0.5
- out_gain: float32 [2, 128], replicated, may hold values from 0.1 to 1.9
- out_weight: bfloat16 [2, 128, 128], replicated, may hold values from -0.5 to 0.5
Outputs:
- result: bfloat16 [6144, 384, 128], P(('graph', 'row')), parts along dimension 0
There are 16 independent parts, one for each index of `graph`. A program takes and returns all parts, laid end to end along the dimension named above; an argument that names none is the same for every part. Nothing has to cross between parts.
All inputs are finite; a program needn't handle non-finite values.
Results may differ from a plain program's by a relative error of at most 0.012.
Values may be sent and summed in bfloat16 or wider, within the bound.
No kernel may reach another device: no remote copies, remote signals or barrier semaphores. Data moves between devices by JAX's collectives and lax.ppermute only.
A program may use at most 64 MiB of HBM per device.

v0:
```python
import jax
import jax.numpy as jnp
from jax import lax
from jax.sharding import PartitionSpec as P


def layer_norm_last(value, gain):
    mean = jnp.mean(value, axis=-1, keepdims=True)
    centered = value - mean
    var = jnp.mean(centered * centered, axis=-1, keepdims=True)
    return centered * lax.rsqrt(var + 1e-05) * gain


def layer_norm_first(value, gain):
    mean = jnp.mean(value, axis=0, keepdims=True)
    centered = value - mean
    var = jnp.mean(centered * centered, axis=0, keepdims=True)
    return centered * lax.rsqrt(var + 1e-05) * gain[:, None, None]


def outgoing_product(left, right):
    return jnp.einsum("gcik,gcjk->gcij", left, right, preferred_element_type=jnp.float32).astype(
        jnp.bfloat16
    )


def incoming_product(left, right):
    return jnp.einsum("gcki,gckj->gcij", left, right, preferred_element_type=jnp.float32).astype(
        jnp.bfloat16
    )


def triangle(left, right, product_fn):
    left_cols, right_cols = (
        lax.all_to_all(left, "row", split_axis=0, concat_axis=2, tiled=True),
        lax.all_to_all(right, "row", split_axis=0, concat_axis=2, tiled=True),
    )
    tri_cols = product_fn(left_cols, right_cols)
    return lax.all_to_all(tri_cols, "row", split_axis=2, concat_axis=0, tiled=True)


def body(
    pair, edge_type, node_mask, type_table, in_gain, proj_weight, gate_weight, out_gain, out_weight
):
    rows, nodes, chans = pair.shape
    hidden = out_weight.shape[1]
    groups = lax.axis_size("row")
    per_group = hidden // groups
    kinds = jnp.arange(type_table.shape[0], dtype=jnp.int32)
    onehot = (edge_type[..., None] == kinds).astype(jnp.bfloat16)
    table_rows = jnp.dot(
        onehot.reshape(rows * nodes, -1), type_table, preferred_element_type=jnp.float32
    )
    z = (pair.astype(jnp.float32) + table_rows.reshape(rows, nodes, chans)).astype(jnp.bfloat16)
    maskf = node_mask.astype(jnp.float32)
    row_start = lax.axis_index("row") * rows
    mask_rows = lax.dynamic_slice_in_dim(maskf, row_start, rows)
    pair_mask = mask_rows[:, None] * maskf[None, :]
    for layer in range(2):
        zf = z.astype(jnp.float32)
        normed = layer_norm_last(zf, in_gain[layer]).astype(jnp.bfloat16)
        proj = jnp.einsum(
            "ch,rnc->hrn", proj_weight[layer], normed, preferred_element_type=jnp.float32
        )
        left = (jax.nn.sigmoid(proj[:hidden]) * proj[hidden : 2 * hidden] * pair_mask[None]).astype(
            jnp.bfloat16
        )
        right = (
            jax.nn.sigmoid(proj[2 * hidden : 3 * hidden]) * proj[3 * hidden :] * pair_mask[None]
        ).astype(jnp.bfloat16)
        left = left.reshape(groups, per_group, rows, nodes)
        right = right.reshape(groups, per_group, rows, nodes)
        product_fn = outgoing_product if layer == 0 else incoming_product
        tri = triangle(left, right, product_fn).reshape(hidden, rows, nodes)
        tri_norm = layer_norm_first(tri.astype(jnp.float32), out_gain[layer]).astype(jnp.bfloat16)
        update = jnp.einsum(
            "hrn,hc->rnc", tri_norm, out_weight[layer], preferred_element_type=jnp.float32
        )
        gate = jax.nn.sigmoid(
            jnp.dot(
                normed.reshape(rows * nodes, chans),
                gate_weight[layer],
                preferred_element_type=jnp.float32,
            )
        )
        z = (zf + gate.reshape(rows, nodes, chans) * update).astype(jnp.bfloat16)
    return z


def solution(mesh):
    in_specs = (
        P(("graph", "row"), None, None),
        P(("graph", "row"), None),
        P("graph"),
        P(),
        P(),
        P(),
        P(),
        P(),
        P(),
    )
    out_specs = P(("graph", "row"), None, None)
    return jax.shard_map(body, mesh=mesh, in_specs=in_specs, out_specs=out_specs, check_vma=False)
```

profile of v0, /device:TPU:1, one launch (start us, length us, event | category | flops | bytes accessed | tf_op | source)
XLA Modules:
  0.0 190.9 jit_solution(15992657056175158366)
XLA Ops:
  0.7 2.6 %convert_reduce_fusion.1 = (f32[12,384]{1,0:T(8,128)S(1)}, bf16[12,384,128]{2,1,0:T(8,128)(2,1)S(1)}) fusion(bf16[8,128]{1,0:T(8,128)(2,1)S(1)} %copy-done, s32[12,384]{1,0:T(8,128)} %param.10, bf16[12,384,128]{2,1,0:T(8,128)(2,1)} %param.9), kind=kOutput, calls=%fused_computation.13 | convolution fusion | flops 12418560 | bytes 2398208 | tf_op jit(solution)/shard_map/dot_general | solution.py:51
  11.7 2.5 %reshape.157 = bf16[32,4,12,384]{3,1,0,2:T(4,128)(2,1)S(1)} reshape(bf16[128,12,384]{2,0,1:T(8,128)(2,1)} %copy.36) | data formatting | bytes 2359296 | tf_op jit(solution)/shard_map/reshape | solution.py:71
  15.6 11.1 %all-to-all-start = ((bf16[32,4,12,384]{3,1,2,0:T(4,128)(2,1)}), bf16[32,4,12,384]{3,1,2,0:T(4,128)(2,1)}, u32[]{:S(2)}, u32[]{:S(2)}) async-start(bf16[32,4,12,384]{3,1,2,0:T(4,128)(2,1)} %copy.37), calls=%async_computation | async-start | bytes 2359296 | tf_op jit(solution)/shard_map/all_to_all | solution.py:35
  28.7 1.7 copy.39
  30.4 14.9 %all-to-all-done = bf16[32,4,12,384]{3,1,2,0:T(4,128)(2,1)} async-done(((bf16[32,4,12,384]{3,1,2,0:T(4,128)(2,1)}), bf16[32,4,12,384]{3,1,2,0:T(4,128)(2,1)}, u32[]{:S(2)}, u32[]{:S(2)}) %all-to-all-start) | async-done | bytes 1179680 | tf_op jit(solution)/shard_map/all_to_all | solution.py:35
  45.3 22.6 %all_to_all.78 = bf16[32,4,12,384]{3,1,2,0:T(4,128)(2,1)S(1)} all-to-all(bf16[32,4,12,384]{3,1,2,0:T(4,128)(2,1)S(1)} %copy.39), channel_id=1, replica_groups=mesh['graph'=16,'row'=32] {'row'}, dimensions={0} | all-to-all | bytes 2359296 | tf_op jit(solution)/shard_map/all_to_all | solution.py:36
  67.9 2.2 %fusion.52 = bf16[1,4,384,384]{3,2,1,0:T(8,128)(2,1)S(1)} fusion(bf16[4,384,384]{2,0,1:T(4,128)(2,1)S(1)} %bitcast.129, bf16[4,384,384]{2,0,1:T(4,128)(2,1)} %bitcast.10), kind=kOutput, calls=%fused_computation.75 | convolution fusion | flops 453574656 | bytes 3538944 | tf_op jit(solution)/shard_map/gcik,gcjk->gcij/dot_general | solution.py:22
  70.1 1.9 %copy.42 = bf16[1,4,384,384]{3,1,0,2:T(4,128)(2,1)} copy(bf16[1,4,384,384]{3,2,1,0:T(8,128)(2,1)S(1)} %fusion.52) | data formatting | bytes 2359296 | tf_op jit(solution)/shard_map/convert_element_type | solution.py:22
  72.1 4.0 %all-to-all-start.2 = ((bf16[1,4,384,384]{3,1,0,2:T(4,128)(2,1)}), bf16[1,4,384,384]{3,1,0,2:T(4,128)(2,1)S(1)}, u32[]{:S(2)}, u32[]{:S(2)}) async-start(bf16[1,4,384,384]{3,1,0,2:T(4,128)(2,1)} %copy.42), calls=%async_computation.2 | async-start | bytes 2359296 | tf_op jit(solution)/shard_map/all_to_all | solution.py:39
  76.8 2.9 %fusion.4 = f32[4608,128]{1,0:T(8,128)} fusion(bf16[4608,128]{1,0:T(8,128)(2,1)S(1)} %bitcast.125, bf16[2,128,128]{2,1,0:T(8,128)(2,1)} %param.15), kind=kOutput, calls=%fused_computation.6 | convolution fusion | flops 152764416 | bytes 3571712 | tf_op jit(solution)/shard_map/dot_general | solution.py:80
  79.7 14.8 %all-to-all-done.2 = bf16[1,4,384,384]{3,1,0,2:T(4,128)(2,1)S(1)} async-done(((bf16[1,4,384,384]{3,1,0,2:T(4,128)(2,1)}), bf16[1,4,384,384]{3,1,0,2:T(4,128)(2,1)S(1)}, u32[]{:S(2)}, u32[]{:S(2)}) %all-to-all-start.2) | async-done | bytes 1179680 | tf_op jit(solution)/shard_map/all_to_all | solution.py:39
  97.4 2.8 %convert_reduce_fusion = (f32[12,384]{1,0:T(8,128)S(1)}, bf16[12,384,128]{2,1,0:T(8,128)(2,1)S(1)}) fusion(f32[12,384,128]{2,1,0:T(8,128)} %bitcast.127, bf16[128,12,384]{2,0,1:T(8,128)(2,1)S(1)} %convert_element_type.101, bf16[2,128,128]{2,1,0:T(8,128)(2,1)} %param.17, bf16[12,384,128]{2,1,0:T(8,128)(2,1)S(1)} %get-tuple-element.14), kind=kOutput, calls=%fused_computation.10 | convolution fusion | flops 154529280 | bytes 5949440 | tf_op jit(solution)/shard_map/hrn,hc->rnc/dot_general | solution.py:76
  101.8 1.5 fusion.12
  108.5 2.5 %reshape.163 = bf16[32,4,12,384]{3,1,0,2:T(4,128)(2,1)S(1)} reshape(bf16[128,12,384]{2,0,1:T(8,128)(2,1)} %copy.45) | data formatting | bytes 2359296 | tf_op jit(solution)/shard_map/reshape | solution.py:71
  112.5 4.5 %all-to-all-start.3 = ((bf16[32,4,12,384]{3,1,2,0:T(4,128)(2,1)}), bf16[32,4,12,384]{3,1,2,0:T(4,128)(2,1)}, u32[]{:S(2)}, u32[]{:S(2)}) async-start(bf16[32,4,12,384]{3,1,2,0:T(4,128)(2,1)} %copy.46), calls=%async_computation.3 | async-start | bytes 2359296 | tf_op jit(solution)/shard_map/all_to_all | solution.py:35
  118.9 1.7 copy.48
  120.6 14.9 %all-to-all-done.3 = bf16[32,4,12,384]{3,1,2,0:T(4,128)(2,1)} async-done(((bf16[32,4,12,384]{3,1,2,0:T(4,128)(2,1)}), bf16[32,4,12,384]{3,1,2,0:T(4,128)(2,1)}, u32[]{:S(2)}, u32[]{:S(2)}) %all-to-all-start.3) | async-done | bytes 1179680 | tf_op jit(solution)/shard_map/all_to_all | solution.py:35
  135.5 22.6 %all_to_all.79 = bf16[32,4,12,384]{3,1,2,0:T(4,128)(2,1)S(1)} all-to-all(bf16[32,4,12,384]{3,1,2,0:T(4,128)(2,1)S(1)} %copy.48), channel_id=1, replica_groups=mesh['graph'=16,'row'=32] {'row'}, dimensions={0} | all-to-all | bytes 2359296 | tf_op jit(solution)/shard_map/all_to_all | solution.py:36
  158.1 2.2 %fusion.53 = bf16[1,4,384,384]{3,2,1,0:T(8,128)(2,1)S(1)} fusion(bf16[4,384,384]{2,0,1:T(4,128)(2,1)S(1)} %bitcast.130, bf16[4,384,384]{2,0,1:T(4,128)(2,1)} %bitcast.29), kind=kOutput, calls=%fused_computation.76 | convolution fusion | flops 453574656 | bytes 3538944 | tf_op jit(solution)/shard_map/gcki,gckj->gcij/dot_general | solution.py:28
  160.3 1.9 %copy.51 = bf16[1,4,384,384]{3,1,0,2:T(4,128)(2,1)} copy(bf16[1,4,384,384]{3,2,1,0:T(8,128)(2,1)S(1)} %fusion.53) | data formatting | bytes 2359296 | tf_op jit(solution)/shard_map/convert_element_type | solution.py:28
  162.2 4.0 %all-to-all-start.5 = ((bf16[1,4,384,384]{3,1,0,2:T(4,128)(2,1)}), bf16[1,4,384,384]{3,1,0,2:T(4,128)(2,1)S(1)}, u32[]{:S(2)}, u32[]{:S(2)}) async-start(bf16[1,4,384,384]{3,1,0,2:T(4,128)(2,1)} %copy.51), calls=%async_computation.5 | async-start | bytes 2359296 | tf_op jit(solution)/shard_map/all_to_all | solution.py:39
  166.9 2.9 %fusion.5 = f32[4608,128]{1,0:T(8,128)} fusion(bf16[4608,128]{1,0:T(8,128)(2,1)S(1)} %bitcast.126, bf16[2,128,128]{2,1,0:T(8,128)(2,1)} %param.15), kind=kOutput, calls=%fused_computation.7 | convolution fusion | flops 152764416 | bytes 3571712 | tf_op jit(solution)/shard_map/dot_general | solution.py:80
  169.9 14.8 %all-to-all-done.5 = bf16[1,4,384,384]{3,1,0,2:T(4,128)(2,1)S(1)} async-done(((bf16[1,4,384,384]{3,1,0,2:T(4,128)(2,1)}), bf16[1,4,384,384]{3,1,0,2:T(4,128)(2,1)S(1)}, u32[]{:S(2)}, u32[]{:S(2)}) %all-to-all-start.5) | async-done | bytes 1179680 | tf_op jit(solution)/shard_map/all_to_all | solution.py:39
  187.7 3.3 %fusion.17 = bf16[12,384,128]{2,1,0:T(8,128)(2,1)} fusion(bf16[12,384,128]{2,1,0:T(8,128)(2,1)S(1)} %get-tuple-element.16, f32[12,384,128]{2,1,0:T(8,128)} %bitcast.128, bf16[128,12,384]{2,0,1:T(8,128)(2,1)S(1)} %convert_element_type.113, bf16[2,128,128]{2,1,0:T(8,128)(2,1)} %param.17), kind=kOutput, calls=%fused_computation.27 | convolution fusion | flops 153354240 | bytes 5931008 | tf_op jit(solution)/shard_map/hrn,hc->rnc/dot_general | solution.py:76
  (70 shorter events, 29.7 us)
Async XLA Ops:
  0.0 0.7 copy-start
  0.0 4.8 %copy-start.13 = (f32[2,128]{1,0:T(2,128)S(1)}, f32[2,128]{1,0:T(2,128)}, u32[]{:S(2)}) copy-start(f32[2,128]{1,0:T(2,128)} %param.13) | copy-start | bytes 3076
  0.0 4.8 %copy-start.12 = (s32[384]{0:T(512)S(1)}, s32[384]{0:T(512)}, u32[]{:S(2)}) copy-start(s32[384]{0:T(512)} %param.11) | copy-start | bytes 4612
  3.3 4.2 %copy-start.6 = (bf16[2,128,512]{2,1,0:T(8,128)(2,1)S(1)}, bf16[2,128,512]{2,1,0:T(8,128)(2,1)}, u32[]{:S(2)}) copy-start(bf16[2,128,512]{2,1,0:T(8,128)(2,1)} %param.14) | copy-start | bytes 786436
  5.0 3.8 %copy-start.8 = (f32[12,384]{1,0:T(8,128)}, f32[12,384]{1,0:T(8,128)S(1)}, u32[]{:S(2)}) copy-start(f32[12,384]{1,0:T(8,128)S(1)} %broadcast_multiply_fusion) | copy-start | bytes 55300
  6.4 1.0 copy-start.2
  15.6 29.7 %all-to-all-start = ((bf16[32,4,12,384]{3,1,2,0:T(4,128)(2,1)}), bf16[32,4,12,384]{3,1,2,0:T(4,128)(2,1)}, u32[]{:S(2)}, u32[]{:S(2)}) async-start(bf16[32,4,12,384]{3,1,2,0:T(4,128)(2,1)} %copy.37), calls=%async_computation | async-start | bytes 2359296 | tf_op jit(solution)/shard_map/all_to_all | solution.py:35
  70.1 6.0 %copy-start.14 = (f32[2,128]{1,0:T(2,128)S(1)}, f32[2,128]{1,0:T(2,128)}, u32[]{:S(2)}) copy-start(f32[2,128]{1,0:T(2,128)} %param.16) | copy-start | bytes 3076
  70.1 6.7 %copy-start.3 = (bf16[12,384,128]{2,1,0:T(8,128)(2,1)S(1)}, bf16[12,384,128]{2,1,0:T(8,128)(2,1)}, u32[]{:S(2)}) copy-start(bf16[12,384,128]{2,1,0:T(8,128)(2,1)} %copy-done.2) | copy-start | bytes 3538948
  72.1 22.4 %all-to-all-start.2 = ((bf16[1,4,384,384]{3,1,0,2:T(4,128)(2,1)}), bf16[1,4,384,384]{3,1,0,2:T(4,128)(2,1)S(1)}, u32[]{:S(2)}, u32[]{:S(2)}) async-start(bf16[1,4,384,384]{3,1,0,2:T(4,128)(2,1)} %copy.42), calls=%async_computation.2 | async-start | bytes 2359296 | tf_op jit(solution)/shard_map/all_to_all | solution.py:39
  79.7 16.1 %copy-start.10 = (f32[32,4]{1,0:T(8,128)S(1)}, f32[32,4]{1,0:T(8,128)}, u32[]{:S(2)}) copy-start(f32[32,4]{1,0:T(8,128)} %mul.172) | copy-start | bytes 1540
  100.3 4.0 %copy-start.7 = (bf16[2,128,512]{2,1,0:T(8,128)(2,1)S(1)}, bf16[2,128,512]{2,1,0:T(8,128)(2,1)}, u32[]{:S(2)}) copy-start(bf16[2,128,512]{2,1,0:T(8,128)(2,1)} %param.14) | copy-start | bytes 786436
  103.3 1.0 copy-start.4
  104.3 1.4 copy-start.9
  112.5 23.0 %all-to-all-start.3 = ((bf16[32,4,12,384]{3,1,2,0:T(4,128)(2,1)}), bf16[32,4,12,384]{3,1,2,0:T(4,128)(2,1)}, u32[]{:S(2)}, u32[]{:S(2)}) async-start(bf16[32,4,12,384]{3,1,2,0:T(4,128)(2,1)} %copy.46), calls=%async_computation.3 | async-start | bytes 2359296 | tf_op jit(solution)/shard_map/all_to_all | solution.py:35
  160.3 6.6 %copy-start.5 = (bf16[12,384,128]{2,1,0:T(8,128)(2,1)S(1)}, bf16[12,384,128]{2,1,0:T(8,128)(2,1)}, u32[]{:S(2)}) copy-start(bf16[12,384,128]{2,1,0:T(8,128)(2,1)} %copy-done.4) | copy-start | bytes 3538948
  162.2 22.4 %all-to-all-start.5 = ((bf16[1,4,384,384]{3,1,0,2:T(4,128)(2,1)}), bf16[1,4,384,384]{3,1,0,2:T(4,128)(2,1)S(1)}, u32[]{:S(2)}, u32[]{:S(2)}) async-start(bf16[1,4,384,384]{3,1,0,2:T(4,128)(2,1)} %copy.51), calls=%async_computation.5 | async-start | bytes 2359296 | tf_op jit(solution)/shard_map/all_to_all | solution.py:39
  169.9 16.1 %copy-start.11 = (f32[32,4]{1,0:T(8,128)S(1)}, f32[32,4]{1,0:T(8,128)}, u32[]{:S(2)}) copy-start(f32[32,4]{1,0:T(8,128)} %mul.189) | copy-start | bytes 1540
  187.6 3.3 %copy-start.1 = (bf16[8,128]{1,0:T(8,128)(2,1)S(1)}, bf16[8,128]{1,0:T(8,128)(2,1)}, u32[]{:S(2)}) copy-start(bf16[8,128]{1,0:T(8,128)(2,1)} %param.12) | copy-start | bytes 6148
where the time goes:
time: 192 us; the launch traced here: 191 us
  waiting for transfers between devices  59.3 us (31%)
  blocking collectives  45.2 us (24%)
  local copies, waits for them, and re-layouts  27.6 us (14%)
  starting transfers between devices  23.6 us (12%)
  matrix products  21.7 us (11%)
  other arithmetic  13 us (7%)
    all_to_all x2, blocking collectives, triangle(): lax.all_to_all(right, 'row', split_axis=0, concat_axis=2, tiled=True)  45.2 us
    all_to_all x2, waiting for transfers between devices, triangle(): lax.all_to_all(left, 'row', split_axis=0, concat_axis=2, tiled=True)  29.8 us
    all_to_all x2, waiting for transfers between devices, triangle(): lax.all_to_all(tri_cols, 'row', split_axis=2, concat_axis=0, tiled=True)  29.5 us
    all_to_all x2, starting transfers between devices, triangle(): lax.all_to_all(left, 'row', split_axis=0, concat_axis=2, tiled=True)  15.6 us
    all_to_all x2, starting transfers between devices, triangle(): lax.all_to_all(tri_cols, 'row', split_axis=2, concat_axis=0, tiled=True)  7.98 us
    reshape x4, local copies, waits for them, and re-layouts, body(): left = left.reshape(groups, per_group, rows, nodes)  7.85 us
    dot_general x2, matrix products, body(): jnp.einsum('hrn,hc->rnc', tri_norm, out_weight[layer], preferred_element_...  6.1 us
    dot_general x2, matrix products, body(): jnp.dot(normed.reshape(rows * nodes, chans), gate_weight[layer], preferre...  5.89 us
  transfers between devices with their start and end apart: 4, of which 4 were waited for; matrix products, arithmetic and copies ran while one was open for 8% of the time, Pallas kernels for 0%

commit v1 on v0

v1 whole, which is shorter than its diff:
```python
import jax
import jax.numpy as jnp
from jax import lax
from jax.experimental import pallas as pl
from jax.experimental.pallas import tpu as pltpu
from jax.sharding import PartitionSpec as P

F32 = jnp.float32
BF16 = jnp.bfloat16
STEP = 4
NT = (((1,), (1,)), ((), ()))
TN = (((0,), (0,)), ((), ()))


def dot(lhs, rhs):
    return jnp.dot(lhs, rhs, preferred_element_type=F32)


def iotas(rows, cols):
    return lax.broadcasted_iota(jnp.int32, (rows, cols), 0), lax.broadcasted_iota(
        jnp.int32, (rows, cols), 1
    )


def eye(n):
    row, col = iotas(n, n)
    return (row == col).astype(BF16)


def swap_matrix(n, outer, inner):
    row, col = iotas(n, n)
    return (col == (row % inner) * outer + row // inner).astype(BF16)


def norm_channels(value, gain):
    chans = value.shape[0]
    mean = jnp.sum(value, axis=0, keepdims=True) * (1.0 / chans)
    centered = value - mean
    var = jnp.sum(centered * centered, axis=0, keepdims=True) * (1.0 / chans)
    return centered * lax.rsqrt(var + 1e-05) * gain


def prepare_in(gain_ref, proj_ref, gain_s, proj_s, layer, groups):
    chans = gain_ref.shape[1]
    wide = proj_ref.shape[1]
    hidden = wide // 4
    per = hidden // groups
    gain = jnp.broadcast_to(gain_ref[layer : layer + 1, :], (chans, chans)).T
    gain_s[...] = jnp.concatenate([gain] * (gain_s.shape[1] // chans), axis=1)
    row, col = iotas(wide, wide)
    kind = row // (2 * hidden)
    group = (row // (2 * per)) % groups
    side = (row // per) % 2
    source = side * (2 * hidden) + kind * hidden + group * per + row % per
    pick = jnp.where(col == source, jnp.where(kind == 0, 0.5, 1.0), 0.0).astype(BF16)
    proj_s[...] = lax.dot_general(pick, proj_ref[...], NT, preferred_element_type=F32).astype(BF16)


def emit_factors(rows_z, first, start_ref, mask_smem, mask_ref, gain_s, proj_s, z_ref, normed_ref, ab_ref, groups):
    nodes = mask_ref.shape[1]
    lane_mask = mask_ref[...].astype(F32) * 0.5
    done = []
    for r, z in enumerate(rows_z):
        z_ref[r] = z
        normed = norm_channels(z.astype(F32), gain_s[...]).astype(BF16)
        normed_ref[r] = normed
        proj = dot(proj_s[...], normed)
        half = proj.shape[0] // 2
        row_mask = mask_smem[start_ref[0] + first + r].astype(F32)
        ab = (jnp.tanh(proj[:half]) + 1.0) * proj[half:] * (lane_mask * row_mask)
        done.append(ab.reshape(groups, half // groups, nodes))
        if r % 2:
            both = jnp.concatenate(done, axis=1).astype(BF16)
            height = both.shape[1]
            ab_ref[:, (r // 2) * height : (r // 2 + 1) * height, :] = both
            done = []


def first_kernel(
    start_ref, mask_smem, pair_ref, edge_ref, mask_ref, table_ref, gain_ref, proj_ref,
    ab_ref, z_ref, normed_ref, gain_s, proj_s,
):
    step = pl.program_id(0)
    groups = ab_ref.shape[0]

    @pl.when(step == 0)
    def _():
        prepare_in(gain_ref, proj_ref.at[0], gain_s, proj_s, 0, groups)

    kinds, chans = table_ref.shape
    nodes = mask_ref.shape[1]
    ident = eye(chans)
    table = table_ref[...]
    rows_z = []
    for r in range(STEP):
        edges = edge_ref[pl.ds(step * STEP + r, 1), :]
        onehot = (lax.broadcasted_iota(jnp.int32, (kinds, nodes), 0) == edges).astype(BF16)
        added = lax.dot_general(table, onehot, TN, preferred_element_type=F32)
        pair = lax.dot_general(ident, pair_ref[r], NT, preferred_element_type=F32)
        rows_z.append((pair + added).astype(BF16))
    emit_factors(rows_z, step * STEP, start_ref, mask_smem, mask_ref, gain_s, proj_s, z_ref, normed_ref, ab_ref, groups)


def prepare_out(gain_ref, weight_ref, gain_s, weight_s, layer):
    chans = gain_ref.shape[1]
    gain = jnp.broadcast_to(gain_ref[layer : layer + 1, :], (chans, chans)).T
    gain_s[...] = jnp.concatenate([gain] * (gain_s.shape[1] // chans), axis=1)
    weight_s[...] = weight_ref[layer].astype(F32).T.astype(BF16)


def updated_rows(tri_ref, z_ref, gate_ref, gain_s, weight_s):
    groups, height, nodes = tri_ref.shape
    per = height // STEP
    eight = 128 // height
    row, col = iotas(128, 128)
    wide = eight * per
    pick = (col == ((row % wide) // per) * height + (row // wide) * per + row % per).astype(BF16)
    parts = [
        dot(pick, tri_ref[q * eight : (q + 1) * eight].reshape(128, nodes))
        for q in range(groups // eight)
    ]
    rows_z = []
    for r in range(STEP):
        tri = jnp.concatenate([p[r * wide : (r + 1) * wide] for p in parts], axis=0)
        tri_norm = norm_channels(tri, gain_s[...]).astype(BF16)
        update = dot(weight_s[...], tri_norm)
        rows_z.append((z_ref[r].astype(F32) + gate_ref[r] * update).astype(BF16))
    return rows_z


def middle_kernel(
    start_ref, mask_smem, tri_ref, zin_ref, gate_ref, mask_ref, out_gain_ref, out_weight_ref, gain_ref, proj_ref,
    ab_ref, z_ref, normed_ref, out_gain_s, out_weight_s, gain_s, proj_s,
):
    step = pl.program_id(0)
    groups = ab_ref.shape[0]

    @pl.when(step == 0)
    def _():
        prepare_out(out_gain_ref, out_weight_ref, out_gain_s, out_weight_s, 0)
        prepare_in(gain_ref, proj_ref.at[1], gain_s, proj_s, 1, groups)

    rows_z = updated_rows(tri_ref, zin_ref, gate_ref, out_gain_s, out_weight_s)
    emit_factors(rows_z, step * STEP, start_ref, mask_smem, mask_ref, gain_s, proj_s, z_ref, normed_ref, ab_ref, groups)


def last_kernel(tri_ref, zin_ref, gate_ref, out_gain_ref, out_weight_ref, result_ref, out_gain_s, out_weight_s):
    @pl.when(pl.program_id(0) == 0)
    def _():
        prepare_out(out_gain_ref, out_weight_ref, out_gain_s, out_weight_s, 1)

    nodes = tri_ref.shape[2]
    ident = eye(nodes)
    for r, z in enumerate(updated_rows(tri_ref, zin_ref, gate_ref, out_gain_s, out_weight_s)):
        result_ref[r] = lax.dot_general(ident, z, NT, preferred_element_type=F32).astype(BF16)


def gate_kernel(normed_ref, weight_ref, gate_ref, *, layer):
    weight = weight_ref[layer].astype(F32).T * 0.5
    weight = weight.astype(BF16)
    for r in range(normed_ref.shape[0]):
        gate_ref[r] = jnp.tanh(dot(weight, normed_ref[r])) * 0.5 + 0.5


def triangle_kernel(ab_ref, tri_ref, sides_s, tri_s, *, layer):
    kinds, nodes, _ = sides_s.shape
    per = kinds // 2
    high = 128 // kinds
    pick = swap_matrix(128, kinds, high)
    for at in range(nodes // high):
        moved = dot(pick, ab_ref[at * 128 : (at + 1) * 128, :]).astype(BF16)
        for kind in range(kinds):
            sides_s[kind, at * high : (at + 1) * high, :] = moved[kind * high : (kind + 1) * high]
    for c in range(per):
        left, right = sides_s[c], sides_s[per + c]
        tri_s[c] = lax.dot_general(
            left, right, NT if layer == 0 else TN, preferred_element_type=F32
        ).astype(BF16)
    low = 128 // per
    back = swap_matrix(128, low, per)
    for at in range(nodes // low):
        stacked = tri_s[:, at * low : (at + 1) * low, :].reshape(128, nodes)
        tri_ref[at * 128 : (at + 1) * 128, :] = dot(back, stacked).astype(BF16)


LIMIT = 32 * 1024 * 1024


def whole(array):
    zeros = (0,) * array.ndim
    return pl.BlockSpec(array.shape, lambda i: zeros)


def body(
    pair, edge_type, node_mask, type_table, in_gain, proj_weight, gate_weight, out_gain, out_weight
):
    rows, nodes, chans = pair.shape
    hidden = out_weight.shape[1]
    groups = lax.axis_size("row")
    per = hidden // groups
    steps = rows // STEP
    start = jnp.full((1,), lax.axis_index("row") * rows, jnp.int32)
    mask = node_mask.reshape(1, nodes)
    smem = pl.BlockSpec(memory_space=pltpu.SMEM)
    params = pltpu.CompilerParams(vmem_limit_bytes=LIMIT)

    def by_row(*shape):
        return pl.BlockSpec((STEP, *shape), lambda i: (i, 0, 0))

    def by_group(height):
        return pl.BlockSpec((groups, height, nodes), lambda i: (0, i, 0))

    emitted = [
        jax.ShapeDtypeStruct((groups, rows * 2 * per, nodes), BF16),
        jax.ShapeDtypeStruct((rows, chans, nodes), BF16),
        jax.ShapeDtypeStruct((rows, chans, nodes), BF16),
    ]
    emitted_specs = [by_group(STEP * 2 * per), by_row(chans, nodes), by_row(chans, nodes)]
    gain_scratch = pltpu.VMEM((chans, nodes), F32)
    in_scratch = [gain_scratch, pltpu.VMEM((4 * hidden, chans), BF16)]
    out_scratch = [gain_scratch, pltpu.VMEM((chans, hidden), BF16)]

    def gate_of(normed, layer):
        return pl.pallas_call(
            lambda *refs: gate_kernel(*refs, layer=layer),
            out_shape=jax.ShapeDtypeStruct((rows, chans, nodes), F32),
            grid=(steps,),
            in_specs=[by_row(chans, nodes), whole(gate_weight)],
            out_specs=by_row(chans, nodes),
            compiler_params=params,
        )(normed, gate_weight)

    def triangle(ab, layer):
        sent = lax.all_to_all(ab, "row", split_axis=0, concat_axis=0, tiled=True)
        tri = pl.pallas_call(
            lambda *refs: triangle_kernel(*refs, layer=layer),
            out_shape=jax.ShapeDtypeStruct((nodes * per, nodes), BF16),
            scratch_shapes=[pltpu.VMEM((2 * per, nodes, nodes), BF16), pltpu.VMEM((per, nodes, nodes), BF16)],
            compiler_params=params,
        )(sent.reshape(nodes * 2 * per, nodes))
        return lax.all_to_all(
            tri.reshape(groups, rows * per, nodes), "row", split_axis=0, concat_axis=0, tiled=True
        )

    ab, z, normed = pl.pallas_call(
        first_kernel,
        out_shape=emitted,
        grid=(steps,),
        in_specs=[
            smem, smem, by_row(nodes, chans), whole(edge_type), whole(mask), whole(type_table), whole(in_gain),
            whole(proj_weight),
        ],
        out_specs=emitted_specs,
        scratch_shapes=in_scratch,
        compiler_params=params,
    )(start, node_mask, pair, edge_type, mask, type_table, in_gain, proj_weight)
    tri = triangle(ab, 0)
    gate = gate_of(normed, 0)
    ab, z, normed = pl.pallas_call(
        middle_kernel,
        out_shape=emitted,
        grid=(steps,),
        in_specs=[
            smem, smem, by_group(STEP * per), by_row(chans, nodes), by_row(chans, nodes), whole(mask),
            whole(out_gain), whole(out_weight), whole(in_gain), whole(proj_weight),
        ],
        out_specs=emitted_specs,
        scratch_shapes=out_scratch + in_scratch,
        compiler_params=params,
    )(start, node_mask, tri, z, gate, mask, out_gain, out_weight, in_gain, proj_weight)
    tri = triangle(ab, 1)
    gate = gate_of(normed, 1)
    return pl.pallas_call(
        last_kernel,
        out_shape=jax.ShapeDtypeStruct((rows, nodes, chans), BF16),
        grid=(steps,),
        in_specs=[
            by_group(STEP * per), by_row(chans, nodes), by_row(chans, nodes), whole(out_gain), whole(out_weight),
        ],
        out_specs=by_row(nodes, chans),
        scratch_shapes=out_scratch,
        compiler_params=params,
    )(tri, z, gate, out_gain, out_weight)


def solution(mesh):
    in_specs = (
        P(("graph", "row"), None, None),
        P(("graph", "row"), None),
        P("graph"),
        P(),
        P(),
        P(),
        P(),
        P(),
        P(),
    )
    out_specs = P(("graph", "row"), None, None)
    return jax.shard_map(body, mesh=mesh, in_specs=in_specs, out_specs=out_specs, check_vma=False)
```

time: 192 us -> 154 us (0.80)
  blocking collectives: 45.2 us -> 76.2 us
  waiting for transfers between devices: 59.3 us -> 30.6 us
  matrix products: 21.7 us -> 0 us
  Pallas kernels: 0 us -> 21 us
  starting transfers between devices: 23.6 us -> 7.55 us
  other arithmetic: 13 us -> 0 us
  local copies, waits for them, and re-layouts: 27.6 us -> 17.1 us
    all_to_all x2, blocking collectives: 45.2 us -> 76.2 us  [triangle(): sent = lax.all_to_all(ab, 'row', split_axis=0, concat_axis=0, tiled=True)]
    all_to_all x4 -> x2, waiting for transfers between devices: 59.3 us -> 30.6 us  [triangle(): lax.all_to_all(tri.reshape(groups, rows * per, nodes), 'row', split_axis=...]
    dot_general x9 -> x0, matrix products: 21.7 us -> none  [the longest x2 6.1 us: body(): jnp.einsum('hrn,hc->rnc', tri_norm, out_weight[layer], preferred_element_...]
    pallas_call x0 -> x7, Pallas kernels: none -> 21 us  [the longest x2 6.01 us: triangle(): pl.pallas_call(lambda *refs: triangle_kernel(*refs, layer=layer), out_sha...]
    all_to_all x4 -> x2, starting transfers between devices: 23.6 us -> 7.55 us  [triangle(): lax.all_to_all(tri.reshape(groups, rows * per, nodes), 'row', split_axis=...]
    unnamed x30 -> x44, local copies, waits for them, and re-layouts: 2.75 us -> 16.4 us
    reshape x8 -> x1, local copies, waits for them, and re-layouts: 13.6 us -> 0.68 us  [body(): mask = node_mask.reshape(1, nodes)]
    convert_element_type x10 -> x0, local copies, waits for them, and re-layouts: 9.78 us -> none  [the longest x2 2.81 us: body(): (jax.nn.sigmoid(proj[:hidden]) * proj[hidden:2 * hidden] * pair_mask[None...]
  transfers between devices with their start and end apart: 4 -> 2, of which waited for: 4 -> 2; matrix products, arithmetic and copies ran while one was open for 8% -> 0% of each run, Pallas kernels for 0% -> 1%
where the time goes in v1:
time: 154 us; the launch traced here: 153 us
  blocking collectives  76.2 us (49%)
  waiting for transfers between devices  30.6 us (20%)
  Pallas kernels  21 us (14%)
  local copies, waits for them, and re-layouts  17.1 us (11%)
  starting transfers between devices  7.55 us (5%)
    all_to_all x2, blocking collectives, triangle(): sent = lax.all_to_all(ab, 'row', split_axis=0, concat_axis=0, tiled=True)  76.2 us
    all_to_all x2, waiting for transfers between devices, triangle(): lax.all_to_all(tri.reshape(groups, rows * per, nodes), 'row', split_axis=...  30.6 us
    unnamed x44, local copies, waits for them, and re-layouts  16.4 us
    all_to_all x2, starting transfers between devices, triangle(): lax.all_to_all(tri.reshape(groups, rows * per, nodes), 'row', split_axis=...  7.55 us
    pallas_call x2, Pallas kernels, triangle(): pl.pallas_call(lambda *refs: triangle_kernel(*refs, layer=layer), out_sha...  6.01 us
    pallas_call x1, Pallas kernels, body(): pl.pallas_call(middle_kernel, out_shape=emitted, grid=(steps,), in_specs=...  5.1 us
    pallas_call x1, Pallas kernels, body(): pl.pallas_call(last_kernel, out_shape=jax.ShapeDtypeStruct((rows, nodes,...  4.02 us
    pallas_call x1, Pallas kernels, body(): pl.pallas_call(first_kernel, out_shape=emitted, grid=(steps,), in_specs=[...  3.86 us
  transfers between devices with their start and end apart: 2, of which 2 were waited for; matrix products, arithmetic and copies ran while one was open for 0% of the time, Pallas kernels for 1%

profile of v1, /device:TPU:1, one launch (start us, length us, event | category | flops | bytes accessed | tf_op | source)
XLA Modules:
  0.0 152.7 jit_solution(16283440635882567839)
XLA Ops:
  0.7 1.3 copy-done.6
  2.0 0.9 copy-done.9
  5.7 3.9 %shard_map.91 = (bf16[32,96,384]{2,1,0:T(8,128)(2,1)S(1)}, bf16[12,128,384]{2,1,0:T(8,128)(2,1)S(1)}, bf16[12,128,384]{2,1,0:T(8,128)(2,1)S(1)}) custom-call(s32[1]{0:T(128)} %bitcast.start_ref, s32[384]{0:T(512)S(1)} %copy-done.16, bf16[12,384,128]{2,1,0:T(8,128)(2,1)S(1)} %copy-done.6, s32[12,384]{1,0:T(8,128)S(1)} %copy-done.15, ...), custom_call_target="tpu_custom_call" | custom-call | tf_op jit(solution)/shard_map/pallas_call | solution.py:245
  9.6 1.0 copy-done.7
  10.6 41.1 %all_to_all.20 = bf16[32,96,384]{2,1,0:T(8,128)(2,1)S(1)} all-to-all(bf16[32,96,384]{2,1,0:T(8,128)(2,1)S(1)} %get-tuple-element.11), channel_id=1, replica_groups=mesh['graph'=16,'row'=32] {'row'}, dimensions={0} | all-to-all | bytes 4718592 | tf_op jit(solution)/shard_map/all_to_all | solution.py:234
  51.7 3.0 %shard_map.92 = bf16[1536,384]{1,0:T(8,128)(2,1)} custom-call(bf16[3072,384]{1,0:T(8,128)(2,1)S(1)} %bitcast.5), custom_call_target="tpu_custom_call" | custom-call | tf_op jit(solution)/shard_map/pallas_call | solution.py:235
  54.7 3.8 %all-to-all-start.1 = ((bf16[32,48,384]{2,1,0:T(8,128)(2,1)}), bf16[32,48,384]{2,1,0:T(8,128)(2,1)S(1)}, u32[]{:S(2)}, u32[]{:S(2)}) async-start(bf16[32,48,384]{2,1,0:T(8,128)(2,1)} %bitcast.2), calls=%async_computation.1 | async-start | bytes 2359296 | tf_op jit(solution)/shard_map/all_to_all | solution.py:241
  58.5 1.3 copy-done.5
  59.8 0.8 copy-done.11
  60.6 1.0 shard_map.93.gate_ref
  61.7 15.3 %all-to-all-done.1.tri_ref = bf16[32,48,384]{2,1,0:T(8,128)(2,1)S(1)} async-done(((bf16[32,48,384]{2,1,0:T(8,128)(2,1)}), bf16[32,48,384]{2,1,0:T(8,128)(2,1)S(1)}, u32[]{:S(2)}, u32[]{:S(2)}) %all-to-all-start.1) | async-done | bytes 1179680 | tf_op jit(solution)/shard_map/all_to_all | solution.py:241
  77.0 1.3 copy-done.8
  78.2 0.9 copy-done.10
  79.2 0.8 copy-done.13
  80.0 5.1 %shard_map.94 = (bf16[32,96,384]{2,1,0:T(8,128)(2,1)S(1)}, bf16[12,128,384]{2,1,0:T(8,128)(2,1)S(1)}, bf16[12,128,384]{2,1,0:T(8,128)(2,1)S(1)}) custom-call(s32[1]{0:T(128)} %bitcast.start_ref, s32[384]{0:T(512)S(1)} %copy-done.17, bf16[32,48,384]{2,1,0:T(8,128)(2,1)S(1)} %all-to-all-done.1.tri_ref, bf16[12,128,384]{2,1,0:T(8,128)(2,1)S(1)} %copy-done.8, ...), custom_call_target="tpu_custom_call" | custom-call | tf_op jit(solution)/shard_map/pallas_call | solution.py:259
  85.2 1.0 copy-done.2
  86.2 35.1 %all_to_all.21 = bf16[32,96,384]{2,1,0:T(8,128)(2,1)S(1)} all-to-all(bf16[32,96,384]{2,1,0:T(8,128)(2,1)S(1)} %get-tuple-element.14), channel_id=1, replica_groups=mesh['graph'=16,'row'=32] {'row'}, dimensions={0} | all-to-all | bytes 4718592 | tf_op jit(solution)/shard_map/all_to_all | solution.py:234
  121.3 3.0 %shard_map.95 = bf16[1536,384]{1,0:T(8,128)(2,1)} custom-call(bf16[3072,384]{1,0:T(8,128)(2,1)S(1)} %bitcast.6), custom_call_target="tpu_custom_call" | custom-call | tf_op jit(solution)/shard_map/pallas_call | solution.py:235
  124.3 3.8 %all-to-all-start.3 = ((bf16[32,48,384]{2,1,0:T(8,128)(2,1)}), bf16[32,48,384]{2,1,0:T(8,128)(2,1)S(1)}, u32[]{:S(2)}, u32[]{:S(2)}) async-start(bf16[32,48,384]{2,1,0:T(8,128)(2,1)} %bitcast.4), calls=%async_computation.3 | async-start | bytes 2359296 | tf_op jit(solution)/shard_map/all_to_all | solution.py:241
  128.1 1.3 copy-done.3
  130.2 1.0 shard_map.96.gate_ref
  131.2 15.3 %all-to-all-done.3.tri_ref = bf16[32,48,384]{2,1,0:T(8,128)(2,1)S(1)} async-done(((bf16[32,48,384]{2,1,0:T(8,128)(2,1)}), bf16[32,48,384]{2,1,0:T(8,128)(2,1)S(1)}, u32[]{:S(2)}, u32[]{:S(2)}) %all-to-all-start.3) | async-done | bytes 1179680 | tf_op jit(solution)/shard_map/all_to_all | solution.py:241
  146.5 1.3 copy-done.1
  148.6 4.0 %shard_map.97 = bf16[12,384,128]{2,1,0:T(8,128)(2,1)} custom-call(bf16[32,48,384]{2,1,0:T(8,128)(2,1)S(1)} %all-to-all-done.3.tri_ref, bf16[12,128,384]{2,1,0:T(8,128)(2,1)S(1)} %copy-done.1, f32[12,128,384]{2,1,0:T(8,128)S(1)} %shard_map.96.gate_ref, f32[2,128]{1,0:T(2,128)S(1)} %copy-done.20, bf16[2,128,128]{2,1,0:T(8,128)(2,1)S(1)} %copy-done.14), custom_call_target="tpu_custom_call" | custom-call | tf_op jit(solution)/shard_map/pallas_call | solution.py:273
  (34 shorter events, 5.2 us)
Async XLA Ops:
  0.7 1.3 copy-start.6
  2.0 0.9 copy-start.9
  2.9 0.7 copy-start.15
  3.6 0.7 copy-start.16
  4.3 0.7 copy-start.18
  5.0 0.7 copy-start.21
  9.6 1.0 copy-start.7
  10.6 41.1 %copy-start.4 = (bf16[12,128,384]{2,1,0:T(8,128)(2,1)}, bf16[12,128,384]{2,1,0:T(8,128)(2,1)S(1)}, u32[]{:S(2)}) copy-start(bf16[12,128,384]{2,1,0:T(8,128)(2,1)S(1)} %get-tuple-element.13.refs_0_) | copy-start | bytes 3538948
  54.7 22.2 %all-to-all-start.1 = ((bf16[32,48,384]{2,1,0:T(8,128)(2,1)}), bf16[32,48,384]{2,1,0:T(8,128)(2,1)S(1)}, u32[]{:S(2)}, u32[]{:S(2)}) async-start(bf16[32,48,384]{2,1,0:T(8,128)(2,1)} %bitcast.2), calls=%async_computation.1 | async-start | bytes 2359296 | tf_op jit(solution)/shard_map/all_to_all | solution.py:241
  58.5 1.3 copy-start.5
  59.8 0.8 copy-start.11
  60.6 16.3 %copy-start.17 = (s32[384]{0:T(512)S(1)}, s32[384]{0:T(512)}, u32[]{:S(2)}) copy-start(s32[384]{0:T(512)} %mask_smem.3) | copy-start | bytes 4612
  60.6 16.3 %copy-start.19 = (f32[2,128]{1,0:T(2,128)S(1)}, f32[2,128]{1,0:T(2,128)}, u32[]{:S(2)}) copy-start(f32[2,128]{1,0:T(2,128)} %gain_ref.3) | copy-start | bytes 3076
  60.6 16.3 %copy-start.20 = (f32[2,128]{1,0:T(2,128)S(1)}, f32[2,128]{1,0:T(2,128)}, u32[]{:S(2)}) copy-start(f32[2,128]{1,0:T(2,128)} %out_gain_ref.3) | copy-start | bytes 3076
  77.0 1.3 copy-start.8
  78.2 0.9 copy-start.10
  79.2 0.8 copy-start.13
  85.1 1.0 copy-start.2
  86.2 35.1 %copy-start = (bf16[12,128,384]{2,1,0:T(8,128)(2,1)}, bf16[12,128,384]{2,1,0:T(8,128)(2,1)S(1)}, u32[]{:S(2)}) copy-start(bf16[12,128,384]{2,1,0:T(8,128)(2,1)S(1)} %get-tuple-element.15.zin_ref) | copy-start | bytes 3538948
  124.3 22.2 %all-to-all-start.3 = ((bf16[32,48,384]{2,1,0:T(8,128)(2,1)}), bf16[32,48,384]{2,1,0:T(8,128)(2,1)S(1)}, u32[]{:S(2)}, u32[]{:S(2)}) async-start(bf16[32,48,384]{2,1,0:T(8,128)(2,1)} %bitcast.4), calls=%async_computation.3 | async-start | bytes 2359296 | tf_op jit(solution)/shard_map/all_to_all | solution.py:241
  128.1 1.3 copy-start.3
  129.3 0.8 copy-start.12
  146.5 1.3 copy-start.1
  147.8 0.8 copy-start.14

commit v2 on v1

--- a/solution.py
+++ b/solution.py
@@ -57,8 +57,8 @@
 
 
 def emit_factors(rows_z, first, start_ref, mask_smem, mask_ref, gain_s, proj_s, z_ref, normed_ref, ab_ref, groups):
-    nodes = mask_ref.shape[1]
-    lane_mask = mask_ref[...].astype(F32) * 0.5
+    nodes = mask_ref.shape[0]
+    lane_mask = mask_ref[...].reshape(1, nodes).astype(F32) * 0.5
     done = []
     for r, z in enumerate(rows_z):
         z_ref[r] = z
@@ -88,7 +88,7 @@
         prepare_in(gain_ref, proj_ref.at[0], gain_s, proj_s, 0, groups)
 
     kinds, chans = table_ref.shape
-    nodes = mask_ref.shape[1]
+    nodes = mask_ref.shape[0]
     ident = eye(chans)
     table = table_ref[...]
     rows_z = []
@@ -186,6 +186,14 @@
 LIMIT = 32 * 1024 * 1024
 
 
+def in_hbm(array):
+    return pltpu.with_memory_space_constraint(array, pltpu.HBM)
+
+
+def in_vmem(array):
+    return pltpu.with_memory_space_constraint(array, pltpu.VMEM)
+
+
 def whole(array):
     zeros = (0,) * array.ndim
     return pl.BlockSpec(array.shape, lambda i: zeros)
@@ -200,7 +208,7 @@
     per = hidden // groups
     steps = rows // STEP
     start = jnp.full((1,), lax.axis_index("row") * rows, jnp.int32)
-    mask = node_mask.reshape(1, nodes)
+    node_mask = in_hbm(node_mask)
     smem = pl.BlockSpec(memory_space=pltpu.SMEM)
     params = pltpu.CompilerParams(vmem_limit_bytes=LIMIT)
 
@@ -211,10 +219,14 @@
         return pl.BlockSpec((groups, height, nodes), lambda i: (0, i, 0))
 
     emitted = [
-        jax.ShapeDtypeStruct((groups, rows * 2 * per, nodes), BF16),
-        jax.ShapeDtypeStruct((rows, chans, nodes), BF16),
-        jax.ShapeDtypeStruct((rows, chans, nodes), BF16),
+        pltpu.VMEM((groups, rows * 2 * per, nodes), BF16),
+        pltpu.HBM((rows, chans, nodes), BF16),
+        pltpu.HBM((rows, chans, nodes), BF16),
     ]
+    pair, edge_type, type_table, in_gain, proj_weight, gate_weight, out_gain, out_weight = (
+        in_hbm(x)
+        for x in (pair, edge_type, type_table, in_gain, proj_weight, gate_weight, out_gain, out_weight)
+    )
     emitted_specs = [by_group(STEP * 2 * per), by_row(chans, nodes), by_row(chans, nodes)]
     gain_scratch = pltpu.VMEM((chans, nodes), F32)
     in_scratch = [gain_scratch, pltpu.VMEM((4 * hidden, chans), BF16)]
@@ -223,21 +235,21 @@
     def gate_of(normed, layer):
         return pl.pallas_call(
             lambda *refs: gate_kernel(*refs, layer=layer),
-            out_shape=jax.ShapeDtypeStruct((rows, chans, nodes), F32),
+            out_shape=pltpu.HBM((rows, chans, nodes), F32),
             grid=(steps,),
             in_specs=[by_row(chans, nodes), whole(gate_weight)],
             out_specs=by_row(chans, nodes),
             compiler_params=params,
-        )(normed, gate_weight)
+        )(in_hbm(normed), gate_weight)
 
     def triangle(ab, layer):
         sent = lax.all_to_all(ab, "row", split_axis=0, concat_axis=0, tiled=True)
         tri = pl.pallas_call(
             lambda *refs: triangle_kernel(*refs, layer=layer),
-            out_shape=jax.ShapeDtypeStruct((nodes * per, nodes), BF16),
+            out_shape=pltpu.HBM((nodes * per, nodes), BF16),
             scratch_shapes=[pltpu.VMEM((2 * per, nodes, nodes), BF16), pltpu.VMEM((per, nodes, nodes), BF16)],
             compiler_params=params,
-        )(sent.reshape(nodes * 2 * per, nodes))
+        )(in_vmem(sent.reshape(nodes * 2 * per, nodes)))
         return lax.all_to_all(
             tri.reshape(groups, rows * per, nodes), "row", split_axis=0, concat_axis=0, tiled=True
         )
@@ -247,13 +259,13 @@
         out_shape=emitted,
         grid=(steps,),
         in_specs=[
-            smem, smem, by_row(nodes, chans), whole(edge_type), whole(mask), whole(type_table), whole(in_gain),
+            smem, smem, by_row(nodes, chans), whole(edge_type), whole(node_mask), whole(type_table), whole(in_gain),
             whole(proj_weight),
         ],
         out_specs=emitted_specs,
         scratch_shapes=in_scratch,
         compiler_params=params,
-    )(start, node_mask, pair, edge_type, mask, type_table, in_gain, proj_weight)
+    )(start, node_mask, pair, edge_type, node_mask, type_table, in_gain, proj_weight)
     tri = triangle(ab, 0)
     gate = gate_of(normed, 0)
     ab, z, normed = pl.pallas_call(
@@ -261,13 +273,13 @@
         out_shape=emitted,
         grid=(steps,),
         in_specs=[
-            smem, smem, by_group(STEP * per), by_row(chans, nodes), by_row(chans, nodes), whole(mask),
+            smem, smem, by_group(STEP * per), by_row(chans, nodes), by_row(chans, nodes), whole(node_mask),
             whole(out_gain), whole(out_weight), whole(in_gain), whole(proj_weight),
         ],
         out_specs=emitted_specs,
         scratch_shapes=out_scratch + in_scratch,
         compiler_params=params,
-    )(start, node_mask, tri, z, gate, mask, out_gain, out_weight, in_gain, proj_weight)
+    )(start, node_mask, in_vmem(tri), in_hbm(z), in_hbm(gate), node_mask, out_gain, out_weight, in_gain, proj_weight)
     tri = triangle(ab, 1)
     gate = gate_of(normed, 1)
     return pl.pallas_call(
@@ -280,7 +292,7 @@
         out_specs=by_row(nodes, chans),
         scratch_shapes=out_scratch,
         compiler_params=params,
-    )(tri, z, gate, out_gain, out_weight)
+    )(in_vmem(tri), in_hbm(z), in_hbm(gate), out_gain, out_weight)
 
 
 def solution(mesh):

time: 154 us -> 145 us (0.942)
  local copies, waits for them, and re-layouts: 17.1 us -> 0 us
  Pallas kernels: 21 us -> 31.9 us
    unnamed x44 -> x0, local copies, waits for them, and re-layouts: 16.4 us -> none
    pallas_call x2, Pallas kernels: 2.04 us -> 7.74 us  [gate_of(): pl.pallas_call(lambda *refs: gate_kernel(*refs, layer=layer), out_shape=p...]
    pallas_call x1, Pallas kernels: 5.1 us -> 6.95 us  [body(): pl.pallas_call(middle_kernel, out_shape=emitted, grid=(steps,), in_specs=...]
    pallas_call x1, Pallas kernels: 3.86 us -> 5.63 us  [body(): pl.pallas_call(first_kernel, out_shape=emitted, grid=(steps,), in_specs=[...]
  transfers between devices with their start and end apart: 2 -> 2, of which waited for: 2 -> 2; matrix products, arithmetic and copies ran while one was open for 0% -> 0% of each run, Pallas kernels for 1% -> 5%
where the time goes in v2:
time: 145 us
  blocking collectives  76.2 us (53%)
  Pallas kernels  31.9 us (22%)
  waiting for transfers between devices  29.2 us (20%)
  starting transfers between devices  7.55 us (5%)
    all_to_all x2, blocking collectives, triangle(): sent = lax.all_to_all(ab, 'row', split_axis=0, concat_axis=0, tiled=True)  76.2 us
    all_to_all x2, waiting for transfers between devices, triangle(): lax.all_to_all(tri.reshape(groups, rows * per, nodes), 'row', split_axis=...  29.2 us
    pallas_call x2, Pallas kernels, gate_of(): pl.pallas_call(lambda *refs: gate_kernel(*refs, layer=layer), out_shape=p...  7.74 us
    all_to_all x2, starting transfers between devices, triangle(): lax.all_to_all(tri.reshape(groups, rows * per, nodes), 'row', split_axis=...  7.55 us
    pallas_call x1, Pallas kernels, body(): pl.pallas_call(middle_kernel, out_shape=emitted, grid=(steps,), in_specs=...  6.95 us
    pallas_call x2, Pallas kernels, triangle(): pl.pallas_call(lambda *refs: triangle_kernel(*refs, layer=layer), out_sha...  6.02 us
    pallas_call x1, Pallas kernels, body(): pl.pallas_call(first_kernel, out_shape=emitted, grid=(steps,), in_specs=[...  5.63 us
    pallas_call x1, Pallas kernels, body(): pl.pallas_call(last_kernel, out_shape=jax.ShapeDtypeStruct((rows, nodes,...  5.54 us
  transfers between devices with their start and end apart: 2, of which 2 were waited for; matrix products, arithmetic and copies ran while one was open for 0% of the time, Pallas kernels for 5%

profile of v2, /device:TPU:1, one launch (start us, length us, event | category | flops | bytes accessed | tf_op | source)
XLA Modules:
  0.0 144.8 jit_solution(9495611783987204426)
XLA Ops:
  0.0 5.6 %shard_map.91 = (bf16[32,96,384]{2,1,0:T(8,128)(2,1)S(1)}, bf16[12,128,384]{2,1,0:T(8,128)(2,1)}, bf16[12,128,384]{2,1,0:T(8,128)(2,1)}) custom-call(s32[1]{0:T(128)} %bitcast.start_ref, s32[384]{0:T(512)} %mask_ref.3, bf16[12,384,128]{2,1,0:T(8,128)(2,1)} %pair_ref.1, s32[12,384]{1,0:T(8,128)} %edge_ref.1, s32[384]{0:T(512)} %mask_ref.3, ...), custom_call_target="tpu_custom_call" | custom-call | tf_op jit(solution)/shard_map/pallas_call | solution.py:257
  5.6 41.1 %all_to_all.20 = bf16[32,96,384]{2,1,0:T(8,128)(2,1)S(1)} all-to-all(bf16[32,96,384]{2,1,0:T(8,128)(2,1)S(1)} %get-tuple-element.11), channel_id=1, replica_groups=mesh['graph'=16,'row'=32] {'row'}, dimensions={0} | all-to-all | bytes 4718592 | tf_op jit(solution)/shard_map/all_to_all | solution.py:246
  46.7 3.0 %shard_map.92 = bf16[1536,384]{1,0:T(8,128)(2,1)} custom-call(bf16[3072,384]{1,0:T(8,128)(2,1)S(1)} %bitcast.5), custom_call_target="tpu_custom_call" | custom-call | tf_op jit(solution)/shard_map/pallas_call | solution.py:247
  49.7 3.8 %all-to-all-start.1 = ((bf16[32,48,384]{2,1,0:T(8,128)(2,1)}), bf16[32,48,384]{2,1,0:T(8,128)(2,1)S(1)}, u32[]{:S(2)}, u32[]{:S(2)}) async-start(bf16[32,48,384]{2,1,0:T(8,128)(2,1)} %bitcast.7), calls=%async_computation.1 | async-start | bytes 2359296 | tf_op jit(solution)/shard_map/all_to_all | solution.py:253
  53.5 3.9 %shard_map.93.gate_ref = f32[12,128,384]{2,1,0:T(8,128)} custom-call(bf16[12,128,384]{2,1,0:T(8,128)(2,1)} %get-tuple-element.13.refs_0_, bf16[2,128,128]{2,1,0:T(8,128)(2,1)} %refs_1_.3), custom_call_target="tpu_custom_call" | custom-call | tf_op jit(solution)/shard_map/pallas_call | solution.py:236
  57.4 14.6 %all-to-all-done.1.tri_ref = bf16[32,48,384]{2,1,0:T(8,128)(2,1)S(1)} async-done(((bf16[32,48,384]{2,1,0:T(8,128)(2,1)}), bf16[32,48,384]{2,1,0:T(8,128)(2,1)S(1)}, u32[]{:S(2)}, u32[]{:S(2)}) %all-to-all-start.1) | async-done | bytes 1179680 | tf_op jit(solution)/shard_map/all_to_all | solution.py:253
  72.0 7.0 %shard_map.94 = (bf16[32,96,384]{2,1,0:T(8,128)(2,1)S(1)}, bf16[12,128,384]{2,1,0:T(8,128)(2,1)}, bf16[12,128,384]{2,1,0:T(8,128)(2,1)}) custom-call(s32[1]{0:T(128)} %bitcast.start_ref, s32[384]{0:T(512)} %mask_ref.3, bf16[32,48,384]{2,1,0:T(8,128)(2,1)S(1)} %all-to-all-done.1.tri_ref, bf16[12,128,384]{2,1,0:T(8,128)(2,1)} %get-tuple-element.12.zin_ref, ...), custom_call_target="tpu_custom_call" | custom-call | tf_op jit(solution)/shard_map/pallas_call | solution.py:271
  78.9 35.1 %all_to_all.21 = bf16[32,96,384]{2,1,0:T(8,128)(2,1)S(1)} all-to-all(bf16[32,96,384]{2,1,0:T(8,128)(2,1)S(1)} %get-tuple-element.14), channel_id=1, replica_groups=mesh['graph'=16,'row'=32] {'row'}, dimensions={0} | all-to-all | bytes 4718592 | tf_op jit(solution)/shard_map/all_to_all | solution.py:246
  114.1 3.0 %shard_map.95 = bf16[1536,384]{1,0:T(8,128)(2,1)} custom-call(bf16[3072,384]{1,0:T(8,128)(2,1)S(1)} %bitcast.6), custom_call_target="tpu_custom_call" | custom-call | tf_op jit(solution)/shard_map/pallas_call | solution.py:247
  117.0 3.8 %all-to-all-start.3 = ((bf16[32,48,384]{2,1,0:T(8,128)(2,1)}), bf16[32,48,384]{2,1,0:T(8,128)(2,1)S(1)}, u32[]{:S(2)}, u32[]{:S(2)}) async-start(bf16[32,48,384]{2,1,0:T(8,128)(2,1)} %bitcast.8), calls=%async_computation.3 | async-start | bytes 2359296 | tf_op jit(solution)/shard_map/all_to_all | solution.py:253
  120.8 3.9 %shard_map.96.gate_ref = f32[12,128,384]{2,1,0:T(8,128)} custom-call(bf16[12,128,384]{2,1,0:T(8,128)(2,1)} %get-tuple-element.16.refs_0_, bf16[2,128,128]{2,1,0:T(8,128)(2,1)} %refs_1_.3), custom_call_target="tpu_custom_call" | custom-call | tf_op jit(solution)/shard_map/pallas_call | solution.py:236
  124.7 14.6 %all-to-all-done.3.tri_ref = bf16[32,48,384]{2,1,0:T(8,128)(2,1)S(1)} async-done(((bf16[32,48,384]{2,1,0:T(8,128)(2,1)}), bf16[32,48,384]{2,1,0:T(8,128)(2,1)S(1)}, u32[]{:S(2)}, u32[]{:S(2)}) %all-to-all-start.3) | async-done | bytes 1179680 | tf_op jit(solution)/shard_map/all_to_all | solution.py:253
  139.3 5.5 %shard_map.97 = bf16[12,384,128]{2,1,0:T(8,128)(2,1)} custom-call(bf16[32,48,384]{2,1,0:T(8,128)(2,1)S(1)} %all-to-all-done.3.tri_ref, bf16[12,128,384]{2,1,0:T(8,128)(2,1)} %get-tuple-element.15.zin_ref, f32[12,128,384]{2,1,0:T(8,128)} %shard_map.96.gate_ref, f32[2,128]{1,0:T(2,128)} %out_gain_ref.3, bf16[2,128,128]{2,1,0:T(8,128)(2,1)} %out_weight_ref.3), custom_call_target="tpu_custom_call" | custom-call | tf_op jit(solution)/shard_map/pallas_call | solution.py:285
Async XLA Ops:
  49.7 22.2 %all-to-all-start.1 = ((bf16[32,48,384]{2,1,0:T(8,128)(2,1)}), bf16[32,48,384]{2,1,0:T(8,128)(2,1)S(1)}, u32[]{:S(2)}, u32[]{:S(2)}) async-start(bf16[32,48,384]{2,1,0:T(8,128)(2,1)} %bitcast.7), calls=%async_computation.1 | async-start | bytes 2359296 | tf_op jit(solution)/shard_map/all_to_all | solution.py:253
  117.0 22.2 %all-to-all-start.3 = ((bf16[32,48,384]{2,1,0:T(8,128)(2,1)}), bf16[32,48,384]{2,1,0:T(8,128)(2,1)S(1)}, u32[]{:S(2)}, u32[]{:S(2)}) async-start(bf16[32,48,384]{2,1,0:T(8,128)(2,1)} %bitcast.8), calls=%async_computation.3 | async-start | bytes 2359296 | tf_op jit(solution)/shard_map/all_to_all | solution.py:253

commit v3 on v2

v3 whole, which is shorter than its diff:
```python
import jax
import jax.numpy as jnp
from jax import lax
from jax.experimental import pallas as pl
from jax.experimental.pallas import tpu as pltpu
from jax.sharding import PartitionSpec as P

F32 = jnp.float32
BF16 = jnp.bfloat16
STEP = 4
NT = (((1,), (1,)), ((), ()))
TN = (((0,), (0,)), ((), ()))


def dot(lhs, rhs):
    return jnp.dot(lhs, rhs, preferred_element_type=F32)


def iotas(rows, cols):
    return lax.broadcasted_iota(jnp.int32, (rows, cols), 0), lax.broadcasted_iota(
        jnp.int32, (rows, cols), 1
    )


def eye(n):
    row, col = iotas(n, n)
    return (row == col).astype(BF16)


def swap_matrix(n, outer, inner):
    row, col = iotas(n, n)
    return (col == (row % inner) * outer + row // inner).astype(BF16)


def norm_channels(value, gain):
    chans = value.shape[0]
    mean = jnp.sum(value, axis=0, keepdims=True) * (1.0 / chans)
    centered = value - mean
    var = jnp.sum(centered * centered, axis=0, keepdims=True) * (1.0 / chans)
    return centered * lax.rsqrt(var + 1e-05) * gain


def prepare_in(gain_ref, proj_ref, weight_ref, gain_s, proj_s, layer, groups):
    chans = gain_ref.shape[1]
    wide = proj_ref.shape[1]
    hidden = wide // 4
    per = hidden // groups
    gain = jnp.broadcast_to(gain_ref[layer : layer + 1, :], (chans, chans)).T
    gain_s[...] = jnp.concatenate([gain] * (gain_s.shape[1] // chans), axis=1)
    row, col = iotas(2 * hidden, hidden)
    place = col // per * (2 * per) + col % per
    picks = [(row == place + side * per).astype(BF16) for side in range(2)]
    for kind in range(2):
        rows = sum(
            lax.dot_general(
                picks[side], proj_ref[:, (2 * side + kind) * hidden : (2 * side + kind + 1) * hidden], NT,
                preferred_element_type=F32,
            )
            for side in range(2)
        )
        proj_s[2 * kind * hidden : 2 * (kind + 1) * hidden] = (rows * (1.0 - 0.5 * (1 - kind))).astype(BF16)
    proj_s[wide:] = (weight_ref[...].astype(F32).T * 0.5).astype(BF16)


def emit_factors(rows_z, first, own_mask, lane_mask, gain_s, proj_s, ab_ref, z_ref, gate_ref, groups):
    nodes = lane_mask.shape[1]
    done = []
    for r, z in enumerate(rows_z):
        normed = norm_channels(z.astype(F32), gain_s[...]).astype(BF16)
        proj = dot(proj_s[...], normed)
        half = ab_ref.shape[1] // z_ref.shape[0] * groups
        row = first + r
        z_ref[row] = z
        gate_ref[row] = jnp.tanh(proj[2 * half :]) * 0.5 + 0.5
        ab = (jnp.tanh(proj[:half]) + 1.0) * proj[half : 2 * half] * (lane_mask * own_mask[row : row + 1])
        done.append(ab.reshape(groups, half // groups, nodes))
        if r % 2:
            both = jnp.concatenate(done, axis=1).astype(BF16)
            height = both.shape[1]
            ab_ref[:, row // 2 * height : (row // 2 + 1) * height, :] = both
            done = []


def start_all(pairs, sems):
    copies = [pltpu.make_async_copy(source, target, sems.at[i]) for i, (source, target) in enumerate(pairs)]
    for copy in copies:
        copy.start()
    return copies


def chunk(ref, at):
    return ref.at[pl.ds(at * STEP, STEP)]


def row_masks(mask_ref, rows):
    nodes = mask_ref.shape[0]
    lanes = mask_ref[...].reshape(1, nodes).astype(F32)
    row, col = iotas(16, nodes)
    own = jnp.where(col == lax.axis_index("row") * rows + row, lanes, 0.0)
    return jnp.sum(own, axis=1, keepdims=True), lanes * 0.5


def embedded_rows(step, pair_ref, edge_ref, table_ref):
    kinds, chans = table_ref.shape
    nodes = edge_ref.shape[1]
    ident = eye(chans)
    table = table_ref[...]
    rows_z = []
    for r in range(STEP):
        edges = edge_ref[pl.ds(step * STEP + r, 1), :]
        onehot = (lax.broadcasted_iota(jnp.int32, (kinds, nodes), 0) == edges).astype(BF16)
        added = lax.dot_general(table, onehot, TN, preferred_element_type=F32)
        pair = lax.dot_general(ident, pair_ref[r], NT, preferred_element_type=F32)
        rows_z.append((pair + added).astype(BF16))
    return rows_z


def first_kernel(
    pair_hbm, edge_hbm, mask_hbm, table_hbm, gain_hbm, proj_hbm, weight_hbm,
    ab_ref, z_ref, gate_ref,
    pair_ref, edge_ref, mask_ref, table_ref, gain_ref, proj_ref, weight_ref, gain_s, proj_s, sems,
):
    rows, groups = pair_ref.shape[0], ab_ref.shape[0]
    small = [(gain_hbm, gain_ref), (proj_hbm.at[0], proj_ref), (weight_hbm.at[0], weight_ref), (table_hbm, table_ref), (mask_hbm, mask_ref), (edge_hbm, edge_ref)]
    large = [(chunk(pair_hbm, at), chunk(pair_ref, at)) for at in range(rows // STEP)]
    copies = start_all(small + large, sems)
    for copy in copies[:6]:
        copy.wait()
    prepare_in(gain_ref, proj_ref, weight_ref, gain_s, proj_s, 0, groups)
    own_mask, lane_mask = row_masks(mask_ref, rows)
    for at in range(rows // STEP):
        copies[6 + at].wait()
        rows_z = embedded_rows(at, chunk(pair_ref, at), edge_ref, table_ref)
        emit_factors(rows_z, at * STEP, own_mask, lane_mask, gain_s, proj_s, ab_ref, z_ref, gate_ref, groups)


def prepare_out(gain_ref, weight_ref, gain_s, weight_s, layer):
    chans = gain_ref.shape[1]
    gain = jnp.broadcast_to(gain_ref[layer : layer + 1, :], (chans, chans)).T
    gain_s[...] = jnp.concatenate([gain] * (gain_s.shape[1] // chans), axis=1)
    weight_s[...] = weight_ref[...].astype(F32).T.astype(BF16)


def products_of(tri_ref, at):
    groups, _, nodes = tri_ref.shape
    height = STEP * 4
    per = 128 // groups
    eight = 128 // height
    row, col = iotas(128, 128)
    wide = eight * per
    pick = (col == ((row % wide) // per) * height + (row // wide) * per + row % per).astype(BF16)
    parts = [
        dot(pick, tri_ref[q * eight : (q + 1) * eight, at * height : (at + 1) * height, :].reshape(128, nodes))
        for q in range(groups // eight)
    ]
    return [
        jnp.concatenate([p[r * wide : (r + 1) * wide] for p in parts], axis=0) for r in range(STEP)
    ]


def updated_rows(products, z_ref, gate_ref, gain_s, weight_s):
    rows_z = []
    for r, tri in enumerate(products):
        tri_norm = norm_channels(tri, gain_s[...]).astype(BF16)
        update = dot(weight_s[...], tri_norm)
        rows_z.append((z_ref[r].astype(F32) + gate_ref[r].astype(F32) * update).astype(BF16))
    return rows_z


def middle_kernel(
    tri_ref, zin_ref, gin_ref, mask_hbm, out_gain_hbm, out_weight_hbm, gain_hbm, proj_hbm, weight_hbm,
    ab_ref, z_ref, gate_ref,
    mask_ref, out_gain_ref, out_weight_ref, gain_ref, proj_ref, weight_ref,
    out_gain_s, out_weight_s, gain_s, proj_s, sems,
):
    rows, groups = zin_ref.shape[0], ab_ref.shape[0]
    copies = start_all(
        [
            (out_gain_hbm, out_gain_ref), (out_weight_hbm.at[0], out_weight_ref), (gain_hbm, gain_ref),
            (proj_hbm.at[1], proj_ref), (weight_hbm.at[1], weight_ref), (mask_hbm, mask_ref),
        ],
        sems,
    )
    products = products_of(tri_ref, 0)
    for copy in copies:
        copy.wait()
    prepare_out(out_gain_ref, out_weight_ref, out_gain_s, out_weight_s, 0)
    prepare_in(gain_ref, proj_ref, weight_ref, gain_s, proj_s, 1, groups)
    own_mask, lane_mask = row_masks(mask_ref, rows)
    for at in range(rows // STEP):
        if at:
            products = products_of(tri_ref, at)
        rows_z = updated_rows(products, chunk(zin_ref, at), chunk(gin_ref, at), out_gain_s, out_weight_s)
        emit_factors(rows_z, at * STEP, own_mask, lane_mask, gain_s, proj_s, ab_ref, z_ref, gate_ref, groups)


def last_kernel(
    tri_ref, z_ref, gate_ref, out_gain_hbm, out_weight_hbm, result_hbm,
    out_gain_ref, out_weight_ref, result_ref, out_gain_s, out_weight_s, sems, out_sems,
):
    rows = z_ref.shape[0]
    copies = start_all([(out_gain_hbm, out_gain_ref), (out_weight_hbm.at[1], out_weight_ref)], sems)
    products = products_of(tri_ref, 0)
    for copy in copies:
        copy.wait()
    prepare_out(out_gain_ref, out_weight_ref, out_gain_s, out_weight_s, 1)
    ident = eye(tri_ref.shape[2])
    sent = []
    for at in range(rows // STEP):
        if at:
            products = products_of(tri_ref, at)
        rows_z = updated_rows(products, chunk(z_ref, at), chunk(gate_ref, at), out_gain_s, out_weight_s)
        for r, z in enumerate(rows_z):
            result_ref[at * STEP + r] = lax.dot_general(ident, z, NT, preferred_element_type=F32).astype(BF16)
        copy = pltpu.make_async_copy(chunk(result_ref, at), chunk(result_hbm, at), out_sems.at[at])
        copy.start()
        sent.append(copy)
    for copy in sent:
        copy.wait()


def triangle_kernel(ab_ref, tri_ref, sides_s, tri_s, *, layer):
    kinds, nodes, _ = sides_s.shape
    per = kinds // 2
    high = 128 // kinds
    pick = swap_matrix(128, kinds, high)
    for at in range(nodes // high):
        moved = dot(pick, ab_ref[at * 128 : (at + 1) * 128, :]).astype(BF16)
        for kind in range(kinds):
            sides_s[kind, at * high : (at + 1) * high, :] = moved[kind * high : (kind + 1) * high]
    for c in range(per):
        left, right = sides_s[c], sides_s[per + c]
        tri_s[c] = lax.dot_general(
            left, right, NT if layer == 0 else TN, preferred_element_type=F32
        ).astype(BF16)
    low = 128 // per
    back = swap_matrix(128, low, per)
    for at in range(nodes // low):
        stacked = tri_s[:, at * low : (at + 1) * low, :].reshape(128, nodes)
        tri_ref[at * 128 : (at + 1) * 128, :] = dot(back, stacked).astype(BF16)


LIMIT = 32 * 1024 * 1024


def in_hbm(array):
    return pltpu.with_memory_space_constraint(array, pltpu.HBM)


def in_vmem(array):
    return pltpu.with_memory_space_constraint(array, pltpu.VMEM)


def whole(array):
    zeros = (0,) * array.ndim
    return pl.BlockSpec(array.shape, lambda i: zeros)


def body(
    pair, edge_type, node_mask, type_table, in_gain, proj_weight, gate_weight, out_gain, out_weight
):
    rows, nodes, chans = pair.shape
    hidden = out_weight.shape[1]
    groups = lax.axis_size("row")
    per = hidden // groups
    steps = rows // STEP
    node_mask = in_hbm(node_mask)
    params = pltpu.CompilerParams(vmem_limit_bytes=LIMIT)

    def by_row(*shape):
        return pl.BlockSpec((STEP, *shape), lambda i: (i, 0, 0))

    anywhere = pl.BlockSpec(memory_space=pl.ANY)
    vmem = pl.BlockSpec(memory_space=pltpu.VMEM)
    factors = pltpu.VMEM((groups, rows * 2 * per, nodes), BF16)
    emitted = [factors, pltpu.VMEM((rows, chans, nodes), BF16), pltpu.VMEM((rows, chans, nodes), F32)]
    pair, edge_type, type_table, in_gain, proj_weight, gate_weight, out_gain, out_weight = (
        in_hbm(x)
        for x in (pair, edge_type, type_table, in_gain, proj_weight, gate_weight, out_gain, out_weight)
    )
    gain_scratch = pltpu.VMEM((chans, nodes), F32)
    in_scratch = [gain_scratch, pltpu.VMEM((4 * hidden + chans, chans), BF16)]
    out_scratch = [gain_scratch, pltpu.VMEM((chans, hidden), BF16)]
    gains = pltpu.VMEM(in_gain.shape, F32)
    proj_buffer = pltpu.VMEM((chans, 4 * hidden), BF16)
    out_buffer = pltpu.VMEM((hidden, chans), BF16)
    mask_buffer = pltpu.VMEM((nodes,), jnp.int32)

    def sems(count):
        return pltpu.SemaphoreType.DMA((count,))

    def triangle(ab, layer):
        sent = lax.all_to_all(ab, "row", split_axis=0, concat_axis=0, tiled=True)
        tri = pl.pallas_call(
            lambda *refs: triangle_kernel(*refs, layer=layer),
            out_shape=pltpu.VMEM((nodes * per, nodes), BF16),
            in_specs=[vmem],
            out_specs=vmem,
            scratch_shapes=[pltpu.VMEM((2 * per, nodes, nodes), BF16), pltpu.VMEM((per, nodes, nodes), BF16)],
            compiler_params=params,
        )(in_vmem(sent.reshape(nodes * 2 * per, nodes)))
        return lax.all_to_all(
            tri.reshape(groups, rows * per, nodes), "row", split_axis=0, concat_axis=0, tiled=True
        )

    ab, z, gate = pl.pallas_call(
        first_kernel,
        out_shape=emitted,
        in_specs=[anywhere] * 7,
        out_specs=[vmem] * 3,
        scratch_shapes=[
            pltpu.VMEM(pair.shape, BF16), pltpu.VMEM(edge_type.shape, jnp.int32), mask_buffer,
            pltpu.VMEM(type_table.shape, BF16), gains, proj_buffer, out_buffer, *in_scratch, sems(6 + steps),
        ],
        compiler_params=params,
    )(pair, edge_type, node_mask, type_table, in_gain, proj_weight, gate_weight)
    tri = triangle(ab, 0)
    ab, z, gate = pl.pallas_call(
        middle_kernel,
        out_shape=emitted,
        in_specs=[vmem] * 3 + [anywhere] * 6,
        out_specs=[vmem] * 3,
        scratch_shapes=[
            mask_buffer, gains, out_buffer, gains, proj_buffer, out_buffer, *out_scratch, *in_scratch, sems(6),
        ],
        compiler_params=params,
    )(in_vmem(tri), in_vmem(z), in_vmem(gate), node_mask, out_gain, out_weight, in_gain, proj_weight, gate_weight)
    tri = triangle(ab, 1)
    return pl.pallas_call(
        last_kernel,
        out_shape=pltpu.HBM((rows, nodes, chans), BF16),
        in_specs=[vmem] * 3 + [anywhere] * 2,
        out_specs=anywhere,
        scratch_shapes=[
            gains, out_buffer, pltpu.VMEM((rows, nodes, chans), BF16), *out_scratch, sems(2), sems(steps),
        ],
        compiler_params=params,
    )(in_vmem(tri), in_vmem(z), in_vmem(gate), out_gain, out_weight)


def solution(mesh):
    in_specs = (
        P(("graph", "row"), None, None),
        P(("graph", "row"), None),
        P("graph"),
        P(),
        P(),
        P(),
        P(),
        P(),
        P(),
    )
    out_specs = P(("graph", "row"), None, None)
    return jax.shard_map(body, mesh=mesh, in_specs=in_specs, out_specs=out_specs, check_vma=False)
```

time: 145 us -> 138 us (0.952)
  blocking collectives: 76.2 us -> 121 us
  waiting for transfers between devices: 29.2 us -> 0 us
  Pallas kernels: 31.9 us -> 16.9 us
  starting transfers between devices: 7.55 us -> 0 us
    all_to_all x0 -> x2, blocking collectives: none -> 44.8 us  [triangle(): lax.all_to_all(tri.reshape(groups, rows * per, nodes), 'row', split_axis=...]
    all_to_all x2 -> x0, waiting for transfers between devices: 29.2 us -> none  [triangle(): lax.all_to_all(tri.reshape(groups, rows * per, nodes), 'row', split_axis=...]
    pallas_call x5 -> x3, Pallas kernels: 25.9 us -> 13 us  [the longest x1 4.68 us: body(): pl.pallas_call(middle_kernel, out_shape=emitted, in_specs=[vmem] * 3 + [a...]
    all_to_all x2 -> x0, starting transfers between devices: 7.55 us -> none  [triangle(): lax.all_to_all(tri.reshape(groups, rows * per, nodes), 'row', split_axis=...]
    pallas_call x2, Pallas kernels: 6.02 us -> 3.96 us  [triangle(): pl.pallas_call(lambda *refs: triangle_kernel(*refs, layer=layer), out_sha...]
  transfers between devices with their start and end apart: 2 -> 0, of which waited for: 2 -> 0; matrix products, arithmetic and copies ran while one was open for 0% -> 0% of each run, Pallas kernels for 5% -> 0%
where the time goes in v3:
time: 138 us
  blocking collectives  121 us (88%)
  Pallas kernels  16.9 us (12%)
    all_to_all x2, blocking collectives, triangle(): sent = lax.all_to_all(ab, 'row', split_axis=0, concat_axis=0, tiled=True)  76.1 us
    all_to_all x2, blocking collectives, triangle(): lax.all_to_all(tri.reshape(groups, rows * per, nodes), 'row', split_axis=...  44.8 us
    pallas_call x1, Pallas kernels, body(): pl.pallas_call(middle_kernel, out_shape=emitted, in_specs=[vmem] * 3 + [a...  4.68 us
    pallas_call x1, Pallas kernels, body(): pl.pallas_call(first_kernel, out_shape=emitted, in_specs=[anywhere] * 7,...  4.31 us
    pallas_call x1, Pallas kernels, body(): pl.pallas_call(last_kernel, out_shape=pltpu.HBM((rows, nodes, chans), BF1...  3.98 us
    pallas_call x2, Pallas kernels, triangle(): pl.pallas_call(lambda *refs: triangle_kernel(*refs, layer=layer), out_sha...  3.96 us

profile of v3, /device:TPU:1, one launch (start us, length us, event | category | flops | bytes accessed | tf_op | source)
XLA Modules:
  0.0 138.1 jit_solution(11508449049499858123)
XLA Ops:
  0.0 4.3 %shard_map.91 = (bf16[32,96,384]{2,1,0:T(8,128)(2,1)S(1)}, bf16[12,128,384]{2,1,0:T(8,128)(2,1)S(1)}, f32[12,128,384]{2,1,0:T(8,128)S(1)}) custom-call(bf16[12,384,128]{2,1,0:T(8,128)(2,1)} %pair_hbm.1, s32[12,384]{1,0:T(8,128)} %edge_hbm.1, s32[384]{0:T(512)} %mask_hbm.3, bf16[8,128]{1,0:T(8,128)(2,1)} %table_hbm.1, f32[2,128]{1,0:T(2,128)} %gain_hbm.3, ...), custom_call_target="tpu_custom_call" | custom-call | tf_op jit(solution)/shard_map/pallas_call | solution.py:306
  4.3 41.1 %all_to_all.20 = bf16[32,96,384]{2,1,0:T(8,128)(2,1)S(1)} all-to-all(bf16[32,96,384]{2,1,0:T(8,128)(2,1)S(1)} %get-tuple-element.11), channel_id=1, replica_groups=mesh['graph'=16,'row'=32] {'row'}, dimensions={0} | all-to-all | bytes 4718592 | tf_op jit(solution)/shard_map/all_to_all | solution.py:293
  45.4 2.0 %shard_map.92 = bf16[1536,384]{1,0:T(8,128)(2,1)S(1)} custom-call(bf16[3072,384]{1,0:T(8,128)(2,1)S(1)} %bitcast.4), custom_call_target="tpu_custom_call" | custom-call | tf_op jit(solution)/shard_map/pallas_call | solution.py:294
  47.4 22.4 %all_to_all.21.tri_ref = bf16[32,48,384]{2,1,0:T(8,128)(2,1)S(1)} all-to-all(bf16[32,48,384]{2,1,0:T(8,128)(2,1)S(1)} %bitcast.6), channel_id=1, replica_groups=mesh['graph'=16,'row'=32] {'row'}, dimensions={0} | all-to-all | bytes 2359296 | tf_op jit(solution)/shard_map/all_to_all | solution.py:302
  69.8 4.7 %shard_map.93 = (bf16[32,96,384]{2,1,0:T(8,128)(2,1)S(1)}, bf16[12,128,384]{2,1,0:T(8,128)(2,1)S(1)}, f32[12,128,384]{2,1,0:T(8,128)S(1)}) custom-call(bf16[32,48,384]{2,1,0:T(8,128)(2,1)S(1)} %all_to_all.21.tri_ref, bf16[12,128,384]{2,1,0:T(8,128)(2,1)S(1)} %get-tuple-element.12.zin_ref, f32[12,128,384]{2,1,0:T(8,128)S(1)} %get-tuple-element.13.gin_ref, ...), custom_call_target="tpu_custom_call" | custom-call | tf_op jit(solution)/shard_map/pallas_call | solution.py:318
  74.5 35.0 %all_to_all.22 = bf16[32,96,384]{2,1,0:T(8,128)(2,1)S(1)} all-to-all(bf16[32,96,384]{2,1,0:T(8,128)(2,1)S(1)} %get-tuple-element.14), channel_id=1, replica_groups=mesh['graph'=16,'row'=32] {'row'}, dimensions={0} | all-to-all | bytes 4718592 | tf_op jit(solution)/shard_map/all_to_all | solution.py:293
  109.6 2.0 %shard_map.94 = bf16[1536,384]{1,0:T(8,128)(2,1)S(1)} custom-call(bf16[3072,384]{1,0:T(8,128)(2,1)S(1)} %bitcast.5), custom_call_target="tpu_custom_call" | custom-call | tf_op jit(solution)/shard_map/pallas_call | solution.py:294
  111.5 22.4 %all_to_all.23.tri_ref = bf16[32,48,384]{2,1,0:T(8,128)(2,1)S(1)} all-to-all(bf16[32,48,384]{2,1,0:T(8,128)(2,1)S(1)} %bitcast.7), channel_id=1, replica_groups=mesh['graph'=16,'row'=32] {'row'}, dimensions={0} | all-to-all | bytes 2359296 | tf_op jit(solution)/shard_map/all_to_all | solution.py:302
  133.9 4.0 %shard_map.95 = bf16[12,384,128]{2,1,0:T(8,128)(2,1)} custom-call(bf16[32,48,384]{2,1,0:T(8,128)(2,1)S(1)} %all_to_all.23.tri_ref, bf16[12,128,384]{2,1,0:T(8,128)(2,1)S(1)} %get-tuple-element.15.z_ref, f32[12,128,384]{2,1,0:T(8,128)S(1)} %get-tuple-element.16.gate_ref, f32[2,128]{1,0:T(2,128)} %out_gain_hbm.3, bf16[2,128,128]{2,1,0:T(8,128)(2,1)} %out_weight_hbm.3), custom_call_target="tpu_custom_call" | custom-call | tf_op jit(solution)/shard_map/pallas_call | solution.py:329

commit v4 on v3

v4 whole, which is shorter than its diff:
```python
import jax
import jax.numpy as jnp
from jax import lax
from jax.experimental import pallas as pl
from jax.experimental.pallas import tpu as pltpu
from jax.sharding import PartitionSpec as P

F32 = jnp.float32
BF16 = jnp.bfloat16
STEP = 4
NT = (((1,), (1,)), ((), ()))
TN = (((0,), (0,)), ((), ()))


def dot(lhs, rhs):
    return jnp.dot(lhs, rhs, preferred_element_type=F32)


def iotas(rows, cols):
    return lax.broadcasted_iota(jnp.int32, (rows, cols), 0), lax.broadcasted_iota(
        jnp.int32, (rows, cols), 1
    )


def eye(n):
    row, col = iotas(n, n)
    return (row == col).astype(BF16)


def swap_matrix(n, outer, inner):
    row, col = iotas(n, n)
    return (col == (row % inner) * outer + row // inner).astype(BF16)


def norm_channels(value, gain):
    chans = value.shape[0]
    mean = jnp.sum(value, axis=0, keepdims=True) * (1.0 / chans)
    centered = value - mean
    var = jnp.sum(centered * centered, axis=0, keepdims=True) * (1.0 / chans)
    return centered * lax.rsqrt(var + 1e-05) * gain


def prepare_in(gain_ref, proj_ref, weight_ref, gain_s, proj_s, layer, groups):
    chans = gain_ref.shape[1]
    wide = proj_ref.shape[1]
    hidden = wide // 4
    per = hidden // groups
    gain = jnp.broadcast_to(gain_ref[layer : layer + 1, :], (chans, chans)).T
    gain_s[...] = jnp.concatenate([gain] * (gain_s.shape[1] // chans), axis=1)
    row, col = iotas(2 * hidden, hidden)
    place = col // per * (2 * per) + col % per
    picks = [(row == place + side * per).astype(BF16) for side in range(2)]
    for kind in range(2):
        rows = sum(
            lax.dot_general(
                picks[side], proj_ref[:, (2 * side + kind) * hidden : (2 * side + kind + 1) * hidden], NT,
                preferred_element_type=F32,
            )
            for side in range(2)
        )
        proj_s[2 * kind * hidden : 2 * (kind + 1) * hidden] = (rows * (1.0 - 0.5 * (1 - kind))).astype(BF16)
    proj_s[wide:] = (weight_ref[...].astype(F32).T * 0.5).astype(BF16)


def emit_factors(rows_z, first, pair_mask_s, gain_s, proj_s, ab_ref, z_ref, gate_ref, groups):
    nodes = pair_mask_s.shape[1]
    half = ab_ref.shape[1] // z_ref.shape[0] * groups
    for r in range(0, len(rows_z), 2):
        normed = [norm_channels(z.astype(F32), gain_s[...]).astype(BF16) for z in rows_z[r : r + 2]]
        both_rows = dot(proj_s[...], jnp.concatenate(normed, axis=1))
        done = []
        for i in range(2):
            row = first + r + i
            proj = both_rows[:, i * nodes : (i + 1) * nodes]
            z_ref[row] = rows_z[r + i]
            gate_ref[row] = jnp.tanh(proj[2 * half :]) * 0.5 + 0.5
            ab = (jnp.tanh(proj[:half]) + 1.0) * proj[half : 2 * half] * pair_mask_s[row : row + 1, :]
            done.append(ab.reshape(groups, half // groups, nodes))
        both = jnp.concatenate(done, axis=1).astype(BF16)
        height = both.shape[1]
        at = (first + r) // 2 * height
        ab_ref[:, at : at + height, :] = both


def start_all(pairs, sems):
    copies = [pltpu.make_async_copy(source, target, sems.at[i]) for i, (source, target) in enumerate(pairs)]
    for copy in copies:
        copy.start()
    return copies


def chunk(ref, at):
    return ref.at[pl.ds(at * STEP, STEP)]


def row_masks(mask_ref, rows):
    nodes = mask_ref.shape[0]
    lanes = mask_ref[...].reshape(1, nodes).astype(F32)
    row, col = iotas(16, nodes)
    own = jnp.where(col == lax.axis_index("row") * rows + row, lanes, 0.0)
    return jnp.sum(own, axis=1, keepdims=True) * (lanes * 0.5)


def embedded_rows(step, pair_ref, edge_ref, table_ref):
    kinds, chans = table_ref.shape
    nodes = edge_ref.shape[1]
    ident = eye(chans)
    table = table_ref[...]
    rows_z = []
    for r in range(0, STEP, 2):
        edges = jnp.concatenate([edge_ref[pl.ds(step * STEP + r + i, 1), :] for i in range(2)], axis=1)
        onehot = (lax.broadcasted_iota(jnp.int32, (kinds, 2 * nodes), 0) == edges).astype(BF16)
        added = lax.dot_general(table, onehot, TN, preferred_element_type=F32)
        pair = lax.dot_general(
            ident, pair_ref[r : r + 2].reshape(2 * nodes, chans), NT, preferred_element_type=F32
        )
        z = (pair + added).astype(BF16)
        rows_z += [z[:, :nodes], z[:, nodes:]]
    return rows_z


def first_kernel(
    pair_hbm, edge_hbm, mask_hbm, table_hbm, gain_hbm, proj_hbm, weight_hbm, out_gain_hbm, out_weight_hbm,
    ab_ref, z_ref, gate_ref, gain_s, proj_s, pair_mask_s, out_gain_s, out_weight_s,
    pair_ref, edge_ref, mask_ref, table_ref, gain_ref, proj_ref, weight_ref, out_gain_ref, out_weight_ref, sems,
):
    rows, groups = pair_ref.shape[0], ab_ref.shape[0]
    small = [
        (gain_hbm, gain_ref), (proj_hbm, proj_ref), (weight_hbm, weight_ref), (table_hbm, table_ref),
        (mask_hbm, mask_ref), (edge_hbm, edge_ref), (out_gain_hbm, out_gain_ref), (out_weight_hbm, out_weight_ref),
    ]
    large = [(chunk(pair_hbm, at), chunk(pair_ref, at)) for at in range(rows // STEP)]
    copies = start_all(small + large, sems)
    for copy in copies[: len(small)]:
        copy.wait()
    for layer in range(2):
        prepare_in(
            gain_ref, proj_ref.at[layer], weight_ref.at[layer], gain_s.at[layer], proj_s.at[layer], layer, groups
        )
        prepare_out(out_gain_ref, out_weight_ref.at[layer], out_gain_s.at[layer], out_weight_s.at[layer], layer)
    pair_mask_s[...] = row_masks(mask_ref, rows)
    for at in range(rows // STEP):
        copies[len(small) + at].wait()
        rows_z = embedded_rows(at, chunk(pair_ref, at), edge_ref, table_ref)
        emit_factors(rows_z, at * STEP, pair_mask_s, gain_s.at[0], proj_s.at[0], ab_ref, z_ref, gate_ref, groups)


def prepare_out(gain_ref, weight_ref, gain_s, weight_s, layer):
    chans = gain_ref.shape[1]
    gain = jnp.broadcast_to(gain_ref[layer : layer + 1, :], (chans, chans)).T
    gain_s[...] = jnp.concatenate([gain] * (gain_s.shape[1] // chans), axis=1)
    weight_s[...] = weight_ref[...].astype(F32).T.astype(BF16)


def products_of(tri_ref, at):
    groups, _, nodes = tri_ref.shape
    height = STEP * 4
    per = 128 // groups
    eight = 128 // height
    row, col = iotas(128, 128)
    wide = eight * per
    pick = (col == ((row % wide) // per) * height + (row // wide) * per + row % per).astype(BF16)
    blocks = [
        tri_ref[q * eight : (q + 1) * eight, at * height : (at + 1) * height, :].reshape(128, nodes)
        for q in range(groups // eight)
    ]
    parts = []
    for q in range(0, groups // eight, 2):
        moved = dot(pick, jnp.concatenate(blocks[q : q + 2], axis=1))
        parts += [moved[:, :nodes], moved[:, nodes:]]
    return [
        jnp.concatenate([p[r * wide : (r + 1) * wide] for p in parts], axis=0) for r in range(STEP)
    ]


def updated_rows(products, z_ref, gate_ref, gain_s, weight_s):
    rows_z = []
    nodes = z_ref.shape[2]
    for r in range(0, STEP, 2):
        tri_norm = [norm_channels(tri, gain_s[...]).astype(BF16) for tri in products[r : r + 2]]
        update = dot(weight_s[...], jnp.concatenate(tri_norm, axis=1))
        for i in range(2):
            rows_z.append(
                (z_ref[r + i].astype(F32) + gate_ref[r + i] * update[:, i * nodes : (i + 1) * nodes]).astype(BF16)
            )
    return rows_z


def middle_kernel(
    tri_ref, zin_ref, gin_ref, gain_s, proj_s, pair_mask_s, out_gain_s, out_weight_s, ab_ref, z_ref, gate_ref
):
    rows, groups = zin_ref.shape[0], ab_ref.shape[0]
    for at in range(rows // STEP):
        rows_z = updated_rows(
            products_of(tri_ref, at), chunk(zin_ref, at), chunk(gin_ref, at), out_gain_s.at[0], out_weight_s.at[0]
        )
        emit_factors(rows_z, at * STEP, pair_mask_s, gain_s.at[1], proj_s.at[1], ab_ref, z_ref, gate_ref, groups)


def last_kernel(tri_ref, z_ref, gate_ref, out_gain_s, out_weight_s, result_hbm, result_ref, out_sems):
    rows = z_ref.shape[0]
    ident = eye(tri_ref.shape[2])
    sent = []
    for at in range(rows // STEP):
        rows_z = updated_rows(
            products_of(tri_ref, at), chunk(z_ref, at), chunk(gate_ref, at), out_gain_s.at[1], out_weight_s.at[1]
        )
        for r in range(0, STEP, 2):
            turned = lax.dot_general(
                ident, jnp.concatenate(rows_z[r : r + 2], axis=0), NT, preferred_element_type=F32
            ).astype(BF16)
            chans = turned.shape[1] // 2
            result_ref[at * STEP + r] = turned[:, :chans]
            result_ref[at * STEP + r + 1] = turned[:, chans:]
        copy = pltpu.make_async_copy(chunk(result_ref, at), chunk(result_hbm, at), out_sems.at[at])
        copy.start()
        sent.append(copy)
    for copy in sent:
        copy.wait()


def triangle_kernel(ab_ref, tri_ref, sides_s, tri_s, *, layer):
    kinds, nodes, _ = sides_s.shape
    per = kinds // 2
    high = 128 // kinds
    pick = swap_matrix(128, kinds, high)
    for at in range(nodes // high):
        moved = dot(pick, ab_ref[at * 128 : (at + 1) * 128, :]).astype(BF16)
        for kind in range(kinds):
            sides_s[kind, at * high : (at + 1) * high, :] = moved[kind * high : (kind + 1) * high]
    for c in range(per):
        left, right = sides_s[c], sides_s[per + c]
        tri_s[c] = lax.dot_general(
            left, right, NT if layer == 0 else TN, preferred_element_type=F32
        ).astype(BF16)
    low = 128 // per
    back = swap_matrix(128, low, per)
    for at in range(nodes // low):
        stacked = tri_s[:, at * low : (at + 1) * low, :].reshape(128, nodes)
        tri_ref[at * 128 : (at + 1) * 128, :] = dot(back, stacked).astype(BF16)


LIMIT = 32 * 1024 * 1024


def in_hbm(array):
    return pltpu.with_memory_space_constraint(array, pltpu.HBM)


def in_vmem(array):
    return pltpu.with_memory_space_constraint(array, pltpu.VMEM)


def whole(array):
    zeros = (0,) * array.ndim
    return pl.BlockSpec(array.shape, lambda i: zeros)


def body(
    pair, edge_type, node_mask, type_table, in_gain, proj_weight, gate_weight, out_gain, out_weight
):
    rows, nodes, chans = pair.shape
    hidden = out_weight.shape[1]
    groups = lax.axis_size("row")
    per = hidden // groups
    steps = rows // STEP
    node_mask = in_hbm(node_mask)
    params = pltpu.CompilerParams(vmem_limit_bytes=LIMIT)

    def by_row(*shape):
        return pl.BlockSpec((STEP, *shape), lambda i: (i, 0, 0))

    anywhere = pl.BlockSpec(memory_space=pl.ANY)
    vmem = pl.BlockSpec(memory_space=pltpu.VMEM)
    factors = pltpu.VMEM((groups, rows * 2 * per, nodes), BF16)
    emitted = [factors, pltpu.VMEM((rows, chans, nodes), BF16), pltpu.VMEM((rows, chans, nodes), F32)]
    pair, edge_type, type_table, in_gain, proj_weight, gate_weight, out_gain, out_weight = (
        in_hbm(x)
        for x in (pair, edge_type, type_table, in_gain, proj_weight, gate_weight, out_gain, out_weight)
    )
    prepared = [
        pltpu.VMEM((2, chans, nodes), F32), pltpu.VMEM((2, 4 * hidden + chans, chans), BF16),
        pltpu.VMEM((16, nodes), F32), pltpu.VMEM((2, hidden, nodes), F32), pltpu.VMEM((2, chans, hidden), BF16),
    ]

    def sems(count):
        return pltpu.SemaphoreType.DMA((count,))

    def triangle(ab, layer):
        sent = lax.all_to_all(ab, "row", split_axis=0, concat_axis=0, tiled=True)
        tri = pl.pallas_call(
            lambda *refs: triangle_kernel(*refs, layer=layer),
            out_shape=pltpu.VMEM((nodes * per, nodes), BF16),
            in_specs=[vmem],
            out_specs=vmem,
            scratch_shapes=[pltpu.VMEM((2 * per, nodes, nodes), BF16), pltpu.VMEM((per, nodes, nodes), BF16)],
            compiler_params=params,
        )(in_vmem(sent.reshape(nodes * 2 * per, nodes)))
        return lax.all_to_all(
            tri.reshape(groups, rows * per, nodes), "row", split_axis=0, concat_axis=0, tiled=True
        )

    arguments = (
        pair, edge_type, node_mask, type_table, in_gain, proj_weight, gate_weight, out_gain, out_weight
    )
    ab, z, gate, *weights = pl.pallas_call(
        first_kernel,
        out_shape=emitted + prepared,
        in_specs=[anywhere] * 9,
        out_specs=[vmem] * 8,
        scratch_shapes=[*(pltpu.VMEM(x.shape, x.dtype) for x in arguments), sems(8 + steps)],
        compiler_params=params,
    )(*arguments)
    weights = [in_vmem(x) for x in weights]
    tri = triangle(ab, 0)
    ab, z, gate = pl.pallas_call(
        middle_kernel,
        out_shape=emitted,
        in_specs=[vmem] * 8,
        out_specs=[vmem] * 3,
        compiler_params=params,
    )(in_vmem(tri), in_vmem(z), in_vmem(gate), *weights)
    tri = triangle(ab, 1)
    return pl.pallas_call(
        last_kernel,
        out_shape=pltpu.HBM((rows, nodes, chans), BF16),
        in_specs=[vmem] * 5,
        out_specs=anywhere,
        scratch_shapes=[pltpu.VMEM((rows, nodes, chans), BF16), sems(steps)],
        compiler_params=params,
    )(in_vmem(tri), in_vmem(z), in_vmem(gate), *weights[3:])


def solution(mesh):
    in_specs = (
        P(("graph", "row"), None, None),
        P(("graph", "row"), None),
        P("graph"),
        P(),
        P(),
        P(),
        P(),
        P(),
        P(),
    )
    out_specs = P(("graph", "row"), None, None)
    return jax.shard_map(body, mesh=mesh, in_specs=in_specs, out_specs=out_specs, check_vma=False)
```

time: 138 us -> 137 us (level)
  no operation moved by 1% of the time
where the time goes in v4:
time: 137 us
  blocking collectives  121 us (88%)
  Pallas kernels  16 us (12%)
    all_to_all x2, blocking collectives, triangle(): sent = lax.all_to_all(ab, 'row', split_axis=0, concat_axis=0, tiled=True)  76.1 us
    all_to_all x2, blocking collectives, triangle(): lax.all_to_all(tri.reshape(groups, rows * per, nodes), 'row', split_axis=...  44.8 us
    pallas_call x1, Pallas kernels, body(): pl.pallas_call(first_kernel, out_shape=emitted + prepared, in_specs=[anyw...  4.76 us
    pallas_call x2, Pallas kernels, triangle(): pl.pallas_call(lambda *refs: triangle_kernel(*refs, layer=layer), out_sha...  3.97 us
    pallas_call x1, Pallas kernels, body(): pl.pallas_call(middle_kernel, out_shape=emitted, in_specs=[vmem] * 8, out...  3.96 us
    pallas_call x1, Pallas kernels, body(): pl.pallas_call(last_kernel, out_shape=pltpu.HBM((rows, nodes, chans), BF1...  3.3 us

profile of v4, /device:TPU:1, one launch (start us, length us, event | category | flops | bytes accessed | tf_op | source)
XLA Modules:
  0.0 137.1 jit_solution(7578712800615557387)
XLA Ops:
  0.0 4.8 %shard_map.91 = (bf16[32,96,384]{2,1,0:T(8,128)(2,1)S(1)}, bf16[12,128,384]{2,1,0:T(8,128)(2,1)S(1)}, f32[12,128,384]{2,1,0:T(8,128)S(1)}, f32[2,128,384]{2,1,0:...) custom-call(bf16[12,384,128]{2,1,0:T(8,128)(2,1)} %pair_hbm.1, ...), custom_call_target="tpu_custom_call" | custom-call | tf_op jit(solution)/shard_map/pallas_call | solution.py:306
  4.8 41.1 %all_to_all.20 = bf16[32,96,384]{2,1,0:T(8,128)(2,1)S(1)} all-to-all(bf16[32,96,384]{2,1,0:T(8,128)(2,1)S(1)} %get-tuple-element.16), channel_id=1, replica_groups=mesh['graph'=16,'row'=32] {'row'}, dimensions={0} | all-to-all | bytes 4718592 | tf_op jit(solution)/shard_map/all_to_all | solution.py:290
  45.9 2.0 %shard_map.92 = bf16[1536,384]{1,0:T(8,128)(2,1)S(1)} custom-call(bf16[3072,384]{1,0:T(8,128)(2,1)S(1)} %bitcast.4), custom_call_target="tpu_custom_call" | custom-call | tf_op jit(solution)/shard_map/pallas_call | solution.py:291
  47.9 22.4 %all_to_all.21.tri_ref = bf16[32,48,384]{2,1,0:T(8,128)(2,1)S(1)} all-to-all(bf16[32,48,384]{2,1,0:T(8,128)(2,1)S(1)} %bitcast.6), channel_id=1, replica_groups=mesh['graph'=16,'row'=32] {'row'}, dimensions={0} | all-to-all | bytes 2359296 | tf_op jit(solution)/shard_map/all_to_all | solution.py:299
  70.3 4.0 %shard_map.93 = (bf16[32,96,384]{2,1,0:T(8,128)(2,1)S(1)}, bf16[12,128,384]{2,1,0:T(8,128)(2,1)S(1)}, f32[12,128,384]{2,1,0:T(8,128)S(1)}) custom-call(bf16[32,48,384]{2,1,0:T(8,128)(2,1)S(1)} %all_to_all.21.tri_ref, bf16[12,128,384]{2,1,0:T(8,128)(2,1)S(1)} %get-tuple-element.17.zin_ref, f32[12,128,384]{2,1,0:T(8,128)S(1)} %get-tuple-element.18.gin_ref, ...), custom_call_target="tpu_custom_call" | custom-call | tf_op jit(solution)/shard_map/pallas_call | solution.py:316
  74.3 35.0 %all_to_all.22 = bf16[32,96,384]{2,1,0:T(8,128)(2,1)S(1)} all-to-all(bf16[32,96,384]{2,1,0:T(8,128)(2,1)S(1)} %get-tuple-element.24), channel_id=1, replica_groups=mesh['graph'=16,'row'=32] {'row'}, dimensions={0} | all-to-all | bytes 4718592 | tf_op jit(solution)/shard_map/all_to_all | solution.py:290
  109.3 2.0 %shard_map.94 = bf16[1536,384]{1,0:T(8,128)(2,1)S(1)} custom-call(bf16[3072,384]{1,0:T(8,128)(2,1)S(1)} %bitcast.5), custom_call_target="tpu_custom_call" | custom-call | tf_op jit(solution)/shard_map/pallas_call | solution.py:291
  111.3 22.4 %all_to_all.23.tri_ref = bf16[32,48,384]{2,1,0:T(8,128)(2,1)S(1)} all-to-all(bf16[32,48,384]{2,1,0:T(8,128)(2,1)S(1)} %bitcast.7), channel_id=1, replica_groups=mesh['graph'=16,'row'=32] {'row'}, dimensions={0} | all-to-all | bytes 2359296 | tf_op jit(solution)/shard_map/all_to_all | solution.py:299
  133.7 3.3 %shard_map.95 = bf16[12,384,128]{2,1,0:T(8,128)(2,1)} custom-call(bf16[32,48,384]{2,1,0:T(8,128)(2,1)S(1)} %all_to_all.23.tri_ref, bf16[12,128,384]{2,1,0:T(8,128)(2,1)S(1)} %get-tuple-element.25.z_ref, f32[12,128,384]{2,1,0:T(8,128)S(1)} %get-tuple-element.26.gate_ref, f32[2,128,384]{2,1,0:T(8,128)S(1)} %get-tuple-element.22.out_gain_s, ...), custom_call_target="tpu_custom_call" | custom-call | tf_op jit(solution)/shard_map/pallas_call | solution.py:324

commit v5 on v4

--- a/solution.py
+++ b/solution.py
@@ -67,14 +67,19 @@
     half = ab_ref.shape[1] // z_ref.shape[0] * groups
     for r in range(0, len(rows_z), 2):
         normed = [norm_channels(z.astype(F32), gain_s[...]).astype(BF16) for z in rows_z[r : r + 2]]
-        both_rows = dot(proj_s[...], jnp.concatenate(normed, axis=1))
+        half_rows = proj_s.shape[0] - 2 * half
+        masked = [n * pair_mask_s[first + r + i : first + r + i + 1, :].astype(BF16) for i, n in enumerate(normed)]
+        plain = jnp.concatenate(normed, axis=1)
+        gates = dot(proj_s[:half], plain)
+        values = dot(proj_s[half : 2 * half], jnp.concatenate(masked, axis=1))
+        outs = dot(proj_s[2 * half :], plain)
         done = []
         for i in range(2):
             row = first + r + i
-            proj = both_rows[:, i * nodes : (i + 1) * nodes]
+            part = slice(i * nodes, (i + 1) * nodes)
             z_ref[row] = rows_z[r + i]
-            gate_ref[row] = jnp.tanh(proj[2 * half :]) * 0.5 + 0.5
-            ab = (jnp.tanh(proj[:half]) + 1.0) * proj[half : 2 * half] * pair_mask_s[row : row + 1, :]
+            gate_ref[row] = jnp.tanh(outs[:, part]) * 0.5 + 0.5
+            ab = (jnp.tanh(gates[:, part]) + 1.0) * values[:, part]
             done.append(ab.reshape(groups, half // groups, nodes))
         both = jnp.concatenate(done, axis=1).astype(BF16)
         height = both.shape[1]
@@ -101,16 +106,15 @@
     return jnp.sum(own, axis=1, keepdims=True) * (lanes * 0.5)
 
 
-def embedded_rows(step, pair_ref, edge_ref, table_ref):
-    kinds, chans = table_ref.shape
+def embedded_rows(step, pair_ref, edge_ref, table):
+    chans, kinds = table.shape
     nodes = edge_ref.shape[1]
     ident = eye(chans)
-    table = table_ref[...]
     rows_z = []
     for r in range(0, STEP, 2):
         edges = jnp.concatenate([edge_ref[pl.ds(step * STEP + r + i, 1), :] for i in range(2)], axis=1)
         onehot = (lax.broadcasted_iota(jnp.int32, (kinds, 2 * nodes), 0) == edges).astype(BF16)
-        added = lax.dot_general(table, onehot, TN, preferred_element_type=F32)
+        added = dot(table, onehot)
         pair = lax.dot_general(
             ident, pair_ref[r : r + 2].reshape(2 * nodes, chans), NT, preferred_element_type=F32
         )
@@ -138,10 +142,11 @@
             gain_ref, proj_ref.at[layer], weight_ref.at[layer], gain_s.at[layer], proj_s.at[layer], layer, groups
         )
         prepare_out(out_gain_ref, out_weight_ref.at[layer], out_gain_s.at[layer], out_weight_s.at[layer], layer)
+    table = table_ref[...].astype(F32).T.astype(BF16)
     pair_mask_s[...] = row_masks(mask_ref, rows)
     for at in range(rows // STEP):
         copies[len(small) + at].wait()
-        rows_z = embedded_rows(at, chunk(pair_ref, at), edge_ref, table_ref)
+        rows_z = embedded_rows(at, chunk(pair_ref, at), edge_ref, table)
         emit_factors(rows_z, at * STEP, pair_mask_s, gain_s.at[0], proj_s.at[0], ab_ref, z_ref, gate_ref, groups)
 
 
@@ -212,9 +217,10 @@
             chans = turned.shape[1] // 2
             result_ref[at * STEP + r] = turned[:, :chans]
             result_ref[at * STEP + r + 1] = turned[:, chans:]
-        copy = pltpu.make_async_copy(chunk(result_ref, at), chunk(result_hbm, at), out_sems.at[at])
-        copy.start()
-        sent.append(copy)
+            pair = pl.ds(at * STEP + r, 2)
+            copy = pltpu.make_async_copy(result_ref.at[pair], result_hbm.at[pair], out_sems.at[len(sent)])
+            copy.start()
+            sent.append(copy)
     for copy in sent:
         copy.wait()
 
@@ -326,7 +332,7 @@
         out_shape=pltpu.HBM((rows, nodes, chans), BF16),
         in_specs=[vmem] * 5,
         out_specs=anywhere,
-        scratch_shapes=[pltpu.VMEM((rows, nodes, chans), BF16), sems(steps)],
+        scratch_shapes=[pltpu.VMEM((rows, nodes, chans), BF16), sems(rows // 2)],
         compiler_params=params,
     )(in_vmem(tri), in_vmem(z), in_vmem(gate), *weights[3:])
 

time: 137 us -> 137 us (level)
  no operation moved by 1% of the time
where the time goes in v5:
time: 137 us
  blocking collectives  121 us (88%)
  Pallas kernels  15.7 us (11%)
    all_to_all x2, blocking collectives, triangle(): sent = lax.all_to_all(ab, 'row', split_axis=0, concat_axis=0, tiled=True)  76.1 us
    all_to_all x2, blocking collectives, triangle(): lax.all_to_all(tri.reshape(groups, rows * per, nodes), 'row', split_axis=...  44.8 us
    pallas_call x1, Pallas kernels, body(): pl.pallas_call(first_kernel, out_shape=emitted + prepared, in_specs=[anyw...  4.55 us
    pallas_call x2, Pallas kernels, triangle(): pl.pallas_call(lambda *refs: triangle_kernel(*refs, layer=layer), out_sha...  3.96 us
    pallas_call x1, Pallas kernels, body(): pl.pallas_call(middle_kernel, out_shape=emitted, in_specs=[vmem] * 8, out...  3.87 us
    pallas_call x1, Pallas kernels, body(): pl.pallas_call(last_kernel, out_shape=pltpu.HBM((rows, nodes, chans), BF1...  3.28 us

profile of v5, /device:TPU:1, one launch (start us, length us, event | category | flops | bytes accessed | tf_op | source)
XLA Modules:
  0.0 136.8 jit_solution(16296083370881169543)
XLA Ops:
  0.0 4.6 %shard_map.91 = (bf16[32,96,384]{2,1,0:T(8,128)(2,1)S(1)}, bf16[12,128,384]{2,1,0:T(8,128)(2,1)S(1)}, f32[12,128,384]{2,1,0:T(8,128)S(1)}, f32[2,128,384]{2,1,0:...) custom-call(bf16[12,384,128]{2,1,0:T(8,128)(2,1)} %pair_hbm.1, ...), custom_call_target="tpu_custom_call" | custom-call | tf_op jit(solution)/shard_map/pallas_call | solution.py:312
  4.6 41.1 %all_to_all.20 = bf16[32,96,384]{2,1,0:T(8,128)(2,1)S(1)} all-to-all(bf16[32,96,384]{2,1,0:T(8,128)(2,1)S(1)} %get-tuple-element.16), channel_id=1, replica_groups=mesh['graph'=16,'row'=32] {'row'}, dimensions={0} | all-to-all | bytes 4718592 | tf_op jit(solution)/shard_map/all_to_all | solution.py:296
  45.7 2.0 %shard_map.92 = bf16[1536,384]{1,0:T(8,128)(2,1)S(1)} custom-call(bf16[3072,384]{1,0:T(8,128)(2,1)S(1)} %bitcast.4), custom_call_target="tpu_custom_call" | custom-call | tf_op jit(solution)/shard_map/pallas_call | solution.py:297
  47.7 22.4 %all_to_all.21.tri_ref = bf16[32,48,384]{2,1,0:T(8,128)(2,1)S(1)} all-to-all(bf16[32,48,384]{2,1,0:T(8,128)(2,1)S(1)} %bitcast.6), channel_id=1, replica_groups=mesh['graph'=16,'row'=32] {'row'}, dimensions={0} | all-to-all | bytes 2359296 | tf_op jit(solution)/shard_map/all_to_all | solution.py:305
  70.1 3.9 %shard_map.93 = (bf16[32,96,384]{2,1,0:T(8,128)(2,1)S(1)}, bf16[12,128,384]{2,1,0:T(8,128)(2,1)S(1)}, f32[12,128,384]{2,1,0:T(8,128)S(1)}) custom-call(bf16[32,48,384]{2,1,0:T(8,128)(2,1)S(1)} %all_to_all.21.tri_ref, bf16[12,128,384]{2,1,0:T(8,128)(2,1)S(1)} %get-tuple-element.17.zin_ref, f32[12,128,384]{2,1,0:T(8,128)S(1)} %get-tuple-element.18.gin_ref, ...), custom_call_target="tpu_custom_call" | custom-call | tf_op jit(solution)/shard_map/pallas_call | solution.py:322
  74.0 35.0 %all_to_all.22 = bf16[32,96,384]{2,1,0:T(8,128)(2,1)S(1)} all-to-all(bf16[32,96,384]{2,1,0:T(8,128)(2,1)S(1)} %get-tuple-element.24), channel_id=1, replica_groups=mesh['graph'=16,'row'=32] {'row'}, dimensions={0} | all-to-all | bytes 4718592 | tf_op jit(solution)/shard_map/all_to_all | solution.py:296
  109.0 1.9 %shard_map.94 = bf16[1536,384]{1,0:T(8,128)(2,1)S(1)} custom-call(bf16[3072,384]{1,0:T(8,128)(2,1)S(1)} %bitcast.5), custom_call_target="tpu_custom_call" | custom-call | tf_op jit(solution)/shard_map/pallas_call | solution.py:297
  110.9 22.4 %all_to_all.23.tri_ref = bf16[32,48,384]{2,1,0:T(8,128)(2,1)S(1)} all-to-all(bf16[32,48,384]{2,1,0:T(8,128)(2,1)S(1)} %bitcast.7), channel_id=1, replica_groups=mesh['graph'=16,'row'=32] {'row'}, dimensions={0} | all-to-all | bytes 2359296 | tf_op jit(solution)/shard_map/all_to_all | solution.py:305
  133.4 3.3 %shard_map.95 = bf16[12,384,128]{2,1,0:T(8,128)(2,1)} custom-call(bf16[32,48,384]{2,1,0:T(8,128)(2,1)S(1)} %all_to_all.23.tri_ref, bf16[12,128,384]{2,1,0:T(8,128)(2,1)S(1)} %get-tuple-element.25.z_ref, f32[12,128,384]{2,1,0:T(8,128)S(1)} %get-tuple-element.26.gate_ref, f32[2,128,384]{2,1,0:T(8,128)S(1)} %get-tuple-element.22.out_gain_s, ...), custom_call_target="tpu_custom_call" | custom-call | tf_op jit(solution)/shard_map/pallas_call | solution.py:330
